TPU v7x, 512 devices: a whole 4x8x8 slice. The times are simulated.
512 devices in a mesh: hours: 64 (over z, x, core), region: 8 (over y).
Axes of the slice: x: 4, y: 8, z: 8, core: 2. Of those that a mesh axis runs over, the one named last changes fastest.
Arguments:
- availability: float32 [4096, 16, 1024], P('hours', None, 'region'), may hold values from 0.1 to 1
- demand: float32 [4096, 1024], P('hours', 'region'), may hold values from 2 to 72, as said below
- gen_cost: float32 [16, 1024], P(None, 'region'), may hold values from 0.05 to 1
- cap_cost: float32 [8, 2048], P('region', 'hours'), may hold values from 204.8 to 2048
- owner_map: int32 [8, 2048], P('region'), may hold values from 0 to 2047, each once within a row
- line_ends: int32 [2, 2048], P(None, 'region'), may hold values from 0 to 127
- line_limit: float32 [2048], P('region'), may hold values from 0.5 to 4
- cross_ends: int32 [2, 8, 256], P(None, 'region'), may hold values from 0 to 127
- cross_limit: float32 [8, 256], P('region'), may hold values from 0.5 to 4
- pair_counts: int32 [8, 8], P('region'), may hold values from 0 to 32, as said below
- store_node: int32 [2048], P('region'), may hold values from 0 to 127
- store_energy: float32 [2048], P('region'), may hold values from 0.02 to 0.4
- store_power: float32 [2048], P('region'), may hold values from 0.2 to 2
- price_start: float32 [4096, 1024], P('hours', 'region'), may hold values from -3 to 0.5
Outputs:
- dispatch: float32 [4096, 16, 1024], P('hours', None, 'region')
- capacity: float32 [8, 2048], P('region', 'hours')
- prices: float32 [4096, 1024], P('hours', 'region')
- charge_state: float32 [4096, 2048], P('hours', 'region')
Inputs may be any that keep to these rules, and one draw needn't show every extreme that they name: `demand`: loads are positive. `owner_map`: each row lists every capacity column of its region once. `pair_counts`: cross lines in use among the 32 slots of each ordered pair of regions; a region has none to itself; some pair uses all 32.
All inputs are finite; a program needn't handle non-finite values.
Results may differ from a plain program's by a relative error of at most 0.00018.
Values sent between devices are 32-bit elements; how exact they have to be, the bound alone decides.
A program may use at most 64 MiB of HBM per device.

v0:
```python
import jax
import jax.numpy as jnp
from jax import lax
from jax.sharding import PartitionSpec as P

ITERS = 4


epsilon = 1e-06
highest = lax.Precision.HIGHEST


def shifted(value, axis, steps):
    count = lax.axis_size(axis)
    pairs = [(source, (source + steps) % count) for source in range(count)]
    return lax.ppermute(value, axis, pairs)


def one_hot(indices, labels):
    return (indices[:, None] == labels[None, :]).astype(jnp.float32)


def to_owners(partial_value, owned_cols):
    summed = lax.psum(partial_value, "hours")
    return lax.dynamic_slice_in_dim(summed, lax.axis_index("hours") * owned_cols, owned_cols)


def spread_columns(capacity_bar):
    return lax.all_gather(capacity_bar, "hours", axis=0, tiled=True)


def body(
    availability,
    demand,
    gen_cost,
    cap_cost,
    owner_map,
    line_ends,
    line_limit,
    cross_ends,
    cross_limit,
    pair_counts,
    store_node,
    store_energy,
    store_power,
    price_start,
):
    hour_rows, tech_count, node_count = availability.shape
    region_count = lax.axis_size("region")
    slot_count = cross_limit.shape[1]
    slot_width = slot_count // region_count
    owned_cols = cap_cost.shape[1]
    owner_cols = owner_map[0]
    inverse = jnp.argsort(owner_cols)
    node_ids = jnp.arange(node_count, dtype=jnp.int32)
    line_inc = one_hot(line_ends[1], node_ids) - one_hot(line_ends[0], node_ids)
    store_map = one_hot(store_node, node_ids)
    leave_map = one_hot(cross_ends[0, 0], node_ids)
    slot_ids = jnp.arange(slot_count, dtype=jnp.int32)
    pair_of = slot_ids // slot_width
    region_ids = jnp.arange(region_count, dtype=jnp.int32)
    in_use = jnp.sum(
        jnp.where(pair_of[:, None] == region_ids[None, :], pair_counts[0][None, :], 0), axis=1
    )
    cross_bound = jnp.where(slot_ids % slot_width < in_use, cross_limit[0], 0.0)
    reach_map = one_hot(
        pair_of * node_count + cross_ends[1, 0],
        jnp.arange(region_count * node_count, dtype=jnp.int32),
    )
    column_costs = cap_cost[0]
    col_weight = to_owners(jnp.sum(availability, axis=0).reshape(-1)[owner_cols], owned_cols)
    dispatch = jnp.zeros_like(availability)
    capacity = jnp.zeros((owned_cols,), jnp.float32)
    inner_flow = jnp.zeros((hour_rows, line_limit.shape[0]), jnp.float32)
    cross_flow = jnp.zeros((hour_rows, slot_count), jnp.float32)
    mirror_flow = jnp.zeros((hour_rows, slot_count), jnp.float32)
    discharge = jnp.zeros((hour_rows, store_node.shape[0]), jnp.float32)
    charge = jnp.zeros((hour_rows, store_node.shape[0]), jnp.float32)
    prices = price_start
    cap_duals = jnp.zeros_like(availability)
    store_duals = jnp.zeros((hour_rows, store_node.shape[0]), jnp.float32)
    weight = jnp.float32(1.0)
    for iteration in range(ITERS):
        final_sweep = iteration == ITERS - 1
        primal_step = 0.5 / weight
        far_side = jnp.dot(
            lax.all_gather(prices, "region", axis=1, tiled=True), reach_map.T, precision=highest
        )
        if iteration == 0:
            next_duals = jnp.zeros_like(store_duals)
            cap_pull = jnp.zeros((owned_cols,), jnp.float32)
        else:
            next_row = shifted(store_duals[:1], "hours", -1)
            next_duals = jnp.concatenate([store_duals[1:], next_row], axis=0)
            cap_pull = to_owners(
                jnp.sum(availability * cap_duals, axis=0).reshape(-1)[owner_cols], owned_cols
            )
        dispatch_new = jnp.maximum(
            dispatch - primal_step * (gen_cost[None] + prices[:, None, :] + cap_duals), 0.0
        )
        capacity_new = jnp.maximum(
            capacity - (column_costs - cap_pull) / (weight * col_weight), 0.0
        )
        inner_new = jnp.clip(
            inner_flow - primal_step * jnp.dot(prices, line_inc.T, precision=highest),
            -line_limit,
            line_limit,
        )
        cross_new = jnp.clip(
            cross_flow - primal_step * (far_side - jnp.dot(prices, leave_map.T, precision=highest)),
            -cross_bound,
            cross_bound,
        )
        mirror_new = mirror_flow
        discharge_new = jnp.clip(
            discharge
            - primal_step * (jnp.dot(prices, store_map.T, precision=highest) + store_duals),
            -store_power,
            store_power,
        )
        charge_new = jnp.clip(charge - primal_step * (store_duals - next_duals), 0.0, store_energy)
        if not final_sweep:
            cap_change = capacity_new - capacity
            primal_sq = (
                jnp.sum((dispatch_new - dispatch) ** 2)
                + jnp.sum(cap_change**2)
                + jnp.sum((inner_new - inner_flow) ** 2)
                + jnp.sum((cross_new - cross_flow) ** 2)
                + jnp.sum((discharge_new - discharge) ** 2)
                + jnp.sum((charge_new - charge) ** 2)
            )
            primal_sum = lax.psum(primal_sq, ("hours", "region"))
        dispatch_bar = 2.0 * dispatch_new - dispatch
        capacity_bar = 2.0 * capacity_new - capacity
        inner_bar = 2.0 * inner_new - inner_flow
        cross_bar = 2.0 * cross_new - cross_flow
        discharge_bar = 2.0 * discharge_new - discharge
        charge_bar = 2.0 * charge_new - charge
        capacity_all = spread_columns(capacity_bar)
        cap_dense = capacity_all[inverse].reshape(tech_count, node_count)
        per_dest = jnp.dot(cross_bar, reach_map, precision=highest)
        balance = (
            jnp.sum(dispatch_bar, axis=1)
            + jnp.dot(inner_bar, line_inc, precision=highest)
            + (
                lax.psum_scatter(per_dest, "region", scatter_dimension=1, tiled=True)
                - jnp.dot(cross_bar, leave_map, precision=highest)
            )
            + jnp.dot(discharge_bar, store_map, precision=highest)
            - demand
        )
        prev_row = shifted(charge_bar[-1:], "hours", 1)
        storage_rows = (
            charge_bar - jnp.concatenate([prev_row, charge_bar[:-1]], axis=0) + discharge_bar
        )
        cap_rows = dispatch_bar - availability * cap_dense[None]
        prices_new = prices + weight / (tech_count + 8.0) * balance
        cap_new = jnp.maximum(cap_duals + weight / 2.0 * cap_rows, 0.0)
        store_new = store_duals + weight / 3.0 * storage_rows
        if not final_sweep:
            dual_sq = (
                jnp.sum((prices_new - prices) ** 2)
                + jnp.sum((cap_new - cap_duals) ** 2)
                + jnp.sum((store_new - store_duals) ** 2)
            )
            dual_sum = lax.psum(dual_sq, ("hours", "region"))
            weight = jnp.sqrt(weight * jnp.sqrt((dual_sum + epsilon) / (primal_sum + epsilon)))
        dispatch, capacity, inner_flow, cross_flow = (
            dispatch_new,
            capacity_new,
            inner_new,
            cross_new,
        )
        mirror_flow = mirror_new
        discharge, charge = (discharge_new, charge_new)
        prices, cap_duals, store_duals = (prices_new, cap_new, store_new)
    return (dispatch, capacity[None], prices, charge)


def solution(mesh):
    placed = (
        P("hours", None, "region"),
        P("hours", "region"),
        P(None, "region"),
        P("region", "hours"),
        P("region", None),
        P(None, "region"),
        P("region"),
        P(None, "region", None),
        P("region", None),
        P("region", None),
        P("region"),
        P("region"),
        P("region"),
        P("hours", "region"),
    )
    return jax.shard_map(
        body,
        mesh=mesh,
        in_specs=placed,
        out_specs=(
            P("hours", None, "region"),
            P("region", "hours"),
            P("hours", "region"),
            P("hours", "region"),
        ),
        check_vma=False,
    )
```

profile of v0, /device:TPU:1, one launch (start us, length us, event | category | flops | bytes accessed | tf_op | source)
XLA Modules:
  0.0 1492.0 jit_solution(16780039333863139814)
XLA Ops:
  7.9 4.6 collective-permute-start
  12.6 20.8 %all_gather.21 = f32[64,1024]{1,0:T(8,128)S(1)} all-gather(f32[64,128]{1,0:T(8,128)} %param.27), channel_id=1, replica_groups=mesh['hours'=64,'region'=8] {'region'}, dimensions={1}, use_global_device_ids=true | all-gather | bytes 294912 | tf_op jit(solution)/shard_map/all_gather | solution.py:87
  35.8 1.3 fusion.74
  37.9 11.8 gather_fusion
  49.7 136.4 %psum.70 = f32[2048]{0:T(1024)S(1)} all-reduce(f32[2048]{0:T(1024)S(1)} %gather_fusion), channel_id=1, replica_groups=mesh['hours'=64,'region'=8] {'hours'}, use_global_device_ids=true, to_apply=%region_5.6 | all-reduce | flops 2048 | bytes 16384 | tf_op jit(solution)/shard_map/psum | solution.py:24
  186.2 1.3 dynamic-slice
  188.9 125.5 %all-reduce = f32[2048]{0:T(1024)S(1)} all-reduce(f32[2048]{0:T(1024)S(1)} %multiply_dynamic-update-slice_fusion), channel_id=1, replica_groups=mesh['hours'=64,'region'=8] {'hours'}, use_global_device_ids=true, to_apply=%add | all-reduce | flops 2048 | bytes 16384
  314.5 5.0 sort.17
  319.5 11.8 gather_fusion.1
  331.3 1.1 multiply_reduce_fusion.6
  332.4 11.8 gather_fusion.2
  344.2 1.0 multiply_reduce_fusion.21
  346.2 126.4 %psum.73 = f32[2048]{0:T(1024)S(1)} all-reduce(f32[2048]{0:T(1024)S(1)} %gather_fusion.2), channel_id=1, replica_groups=mesh['hours'=64,'region'=8] {'hours'}, use_global_device_ids=true, to_apply=%region_21.22 | all-reduce | flops 2048 | bytes 16384 | tf_op jit(solution)/shard_map/psum | solution.py:24
  478.1 1.0 fusion.67
  481.9 2.6 collective-permute-start.1
  484.5 94.0 %all-reduce.5 = (f32[]{:T(128)}, f32[]{:T(128)}) all-reduce(f32[]{:T(128)S(6)} %add.309, f32[]{:T(128)S(6)} %add.315), channel_id=1, replica_groups=mesh['hours'=64,'region'=8] {'hours','region'}, use_global_device_ids=true, to_apply=%region_9.10 | all-reduce | flops 2 | bytes 16 | tf_op jit(solution)/shard_map/psum | solution.py:166
  580.0 18.7 %all_gather.23 = f32[64,1024]{1,0:T(8,128)S(1)} all-gather(f32[64,128]{1,0:T(8,128)S(1)} %get-tuple-element.56), channel_id=1, replica_groups=mesh['hours'=64,'region'=8] {'region'}, dimensions={1}, use_global_device_ids=true | all-gather | bytes 294912 | tf_op jit(solution)/shard_map/all_gather | solution.py:87
  598.7 1.0 multiply_reduce_fusion.17
  600.5 132.2 %all-reduce.1 = f32[2048]{0:T(1024)S(1)} all-reduce(f32[2048]{0:T(1024)S(1)} %subtract_dynamic-update-slice_fusion.1), channel_id=1, replica_groups=mesh['hours'=64,'region'=8] {'hours'}, use_global_device_ids=true, to_apply=%add.1 | all-reduce | flops 2048 | bytes 16384
  732.7 11.8 gather_fusion.3
  746.6 0.9 multiply_reduce_fusion.16
  747.5 1.3 fusion.72
  748.9 1.2 multiply_reduce_fusion.3
  750.1 11.8 gather_fusion.4
  761.9 1.9 collective-permute-start.2
  764.1 126.1 %psum.76 = f32[2048]{0:T(1024)S(1)} all-reduce(f32[2048]{0:T(1024)S(1)} %gather_fusion.4), channel_id=1, replica_groups=mesh['hours'=64,'region'=8] {'hours'}, use_global_device_ids=true, to_apply=%region_36.37 | all-reduce | flops 2048 | bytes 16384 | tf_op jit(solution)/shard_map/psum | solution.py:24
  892.8 1.0 multiply_reduce_fusion.15
  895.1 1.0 fusion.63
  898.9 7.6 collective-permute-start.3
  906.5 94.4 %all-reduce.4 = (f32[]{:T(128)}, f32[]{:T(128)}) all-reduce(f32[]{:T(128)S(6)} %add.329, f32[]{:T(128)S(6)} %add.335), channel_id=1, replica_groups=mesh['hours'=64,'region'=8] {'hours','region'}, use_global_device_ids=true, to_apply=%region_24.25 | all-reduce | flops 2 | bytes 16 | tf_op jit(solution)/shard_map/psum | solution.py:166
  1003.1 1.0 multiply_reduce_fusion.12
  1004.2 18.8 %all_gather.25 = f32[64,1024]{1,0:T(8,128)S(1)} all-gather(f32[64,128]{1,0:T(8,128)S(1)} %get-tuple-element.63), channel_id=1, replica_groups=mesh['hours'=64,'region'=8] {'region'}, dimensions={1}, use_global_device_ids=true | all-gather | bytes 294912 | tf_op jit(solution)/shard_map/all_gather | solution.py:87
  1023.8 132.0 %all-reduce.2 = f32[2048]{0:T(1024)S(1)} all-reduce(f32[2048]{0:T(1024)S(1)} %subtract_dynamic-update-slice_fusion), channel_id=1, replica_groups=mesh['hours'=64,'region'=8] {'hours'}, use_global_device_ids=true, to_apply=%add.2 | all-reduce | flops 2048 | bytes 16384
  1155.8 11.8 gather_fusion.5
  1167.6 1.9 collective-permute-start.4
  1170.3 0.9 multiply_reduce_fusion.11
  1171.2 1.3 fusion.70
  1172.6 1.4 multiply_reduce_fusion
  1174.0 11.8 gather_fusion.6
  1186.1 126.1 %psum.79 = f32[2048]{0:T(1024)S(1)} all-reduce(f32[2048]{0:T(1024)S(1)} %gather_fusion.6), channel_id=1, replica_groups=mesh['hours'=64,'region'=8] {'hours'}, use_global_device_ids=true, to_apply=%region_48.49 | all-reduce | flops 2048 | bytes 16384 | tf_op jit(solution)/shard_map/psum | solution.py:24
  1317.0 1.0 fusion.59
  1320.9 7.6 collective-permute-start.5
  1328.5 94.6 %all-reduce.3 = (f32[]{:T(128)}, f32[]{:T(128)}) all-reduce(f32[]{:T(128)S(6)} %add.349, f32[]{:T(128)S(6)} %add.355), channel_id=1, replica_groups=mesh['hours'=64,'region'=8] {'hours','region'}, use_global_device_ids=true, to_apply=%region_39.40 | all-reduce | flops 2 | bytes 16 | tf_op jit(solution)/shard_map/psum | solution.py:166
  1424.6 18.9 %all_gather.27 = f32[64,1024]{1,0:T(8,128)S(1)} all-gather(f32[64,128]{1,0:T(8,128)S(1)} %get-tuple-element.70), channel_id=1, replica_groups=mesh['hours'=64,'region'=8] {'region'}, dimensions={1}, use_global_device_ids=true | all-gather | bytes 294912 | tf_op jit(solution)/shard_map/all_gather | solution.py:87
  1443.8 1.6 subtract_reduce_fusion
  1446.4 1.3 fusion.68
  1449.6 34.0 %reduce-scatter.11.cloned.1.call-done = f32[64,128]{1,0:T(8,128)} async-done(((f32[64,1024]{1,0:T(8,128)}), f32[64,128]{1,0:T(8,128)}) %reduce-scatter.11.cloned.1.call-update) | async-done | bytes 32784 | tf_op jit(solution)/shard_map/reduce_scatter | solution.py:146
  1483.5 1.0 fusion.55
  (102 shorter events, 20.9 us)
Async XLA Ops:
  7.2 470.9 %reduce-scatter.5.cloned.1.call-start = ((), (), s32[]{:S(2)}) async-start(), calls=%async_computation.4 | async-start | bytes 294912 | tf_op jit(solution)/shard_map/reduce_scatter | solution.py:146
  7.9 4.7 copy-start.9
  7.9 467.3 %collective-permute-start = (f32[1,256]{1,0:T(1,128)S(1)}, f32[1,256]{1,0:T(1,128)S(1)}, u32[]{:S(2)}, u32[]{:S(2)}) collective-permute-start(f32[1,256]{1,0:T(1,128)S(1)} %bitcast.122), channel_id=1, source_target_pairs={{0,8},{8,16},{16,24},{24,32},{32,40},{40,48},{48,56},{56,64},{64,7... | collective-permute-start | bytes 3080 | tf_op jit(solution)/shard_map/ppermute | solution.py:16
  33.3 0.7 copy-start.13
  33.3 0.7 copy-start.12
  34.0 0.8 copy-start.1
  34.1 3.8 copy-start
  37.1 858.0 %reduce-scatter.7.cloned.1.call-start = ((), (), s32[]{:S(2)}) async-start(), calls=%async_computation.5 | async-start | bytes 294912 | tf_op jit(solution)/shard_map/reduce_scatter | solution.py:146
  37.1 0.7 copy-start.11
  37.1 0.7 copy-start.5
  37.1 0.7 copy-start.10
  187.4 0.7 copy-start.8
  319.5 11.8 copy-start.3
  346.1 126.5 %copy-start.7 = (f32[256]{0:T(256)S(1)}, f32[256]{0:T(256)}, u32[]{:S(2)}) copy-start(f32[256]{0:T(256)} %param.26) | copy-start | bytes 3076
  475.1 0.7 copy-start.4
  478.0 1.1 copy-start.2
  481.9 262.6 %collective-permute-start.1 = (f32[1,256]{1,0:T(1,128)S(1)}, f32[1,256]{1,0:T(1,128)S(1)}, u32[]{:S(2)}, u32[]{:S(2)}) collective-permute-start(f32[1,256]{1,0:T(1,128)S(1)} %slice.79), channel_id=1, source_target_pairs={{0,504},{8,0},{16,8},{24,16},{32,24},{40,32},{48,40},{56,48},{64,5... | collective-permute-start | bytes 3080 | tf_op jit(solution)/shard_map/ppermute | solution.py:16
  744.5 0.7 copy-start.6
  748.8 568.2 %reduce-scatter.9.cloned.1.call-start = ((), (), s32[]{:S(2)}) async-start(), calls=%async_computation.6 | async-start | bytes 294912 | tf_op jit(solution)/shard_map/reduce_scatter | solution.py:146
  761.9 130.9 %collective-permute-start.2 = (f32[1,256]{1,0:T(1,128)S(1)}, f32[1,256]{1,0:T(1,128)S(1)}, u32[]{:S(2)}, u32[]{:S(2)}) collective-permute-start(f32[1,256]{1,0:T(1,128)S(1)} %slice.80), channel_id=1, source_target_pairs={{0,8},{8,16},{16,24},{24,32},{32,40},{40,48},{48,56},{56,64},{64,7... | collective-permute-start | bytes 3080 | tf_op jit(solution)/shard_map/ppermute | solution.py:16
  898.9 124.1 %collective-permute-start.3 = (f32[1,256]{1,0:T(1,128)S(1)}, f32[1,256]{1,0:T(1,128)S(1)}, u32[]{:S(2)}, u32[]{:S(2)}) collective-permute-start(f32[1,256]{1,0:T(1,128)S(1)} %slice.83), channel_id=1, source_target_pairs={{0,504},{8,0},{16,8},{24,16},{32,24},{40,32},{48,40},{56,48},{64,5... | collective-permute-start | bytes 3080 | tf_op jit(solution)/shard_map/ppermute | solution.py:16
  1167.6 147.1 %collective-permute-start.4 = (f32[1,256]{1,0:T(1,128)S(1)}, f32[1,256]{1,0:T(1,128)S(1)}, u32[]{:S(2)}, u32[]{:S(2)}) collective-permute-start(f32[1,256]{1,0:T(1,128)S(1)} %slice.84), channel_id=1, source_target_pairs={{0,8},{8,16},{16,24},{24,32},{32,40},{40,48},{48,56},{56,64},{64,7... | collective-permute-start | bytes 3080 | tf_op jit(solution)/shard_map/ppermute | solution.py:16
  1172.5 311.0 %reduce-scatter.11.cloned.1.call-start = ((), (), s32[]{:S(2)}) async-start(), calls=%async_computation.7 | async-start | bytes 294912 | tf_op jit(solution)/shard_map/reduce_scatter | solution.py:146
  1320.9 127.8 %collective-permute-start.5 = (f32[1,256]{1,0:T(1,128)S(1)}, f32[1,256]{1,0:T(1,128)S(1)}, u32[]{:S(2)}, u32[]{:S(2)}) collective-permute-start(f32[1,256]{1,0:T(1,128)S(1)} %slice.87), channel_id=1, source_target_pairs={{0,504},{8,0},{16,8},{24,16},{32,24},{40,32},{48,40},{56,48},{64,5... | collective-permute-start | bytes 3080 | tf_op jit(solution)/shard_map/ppermute | solution.py:16
Sparse Core Ops, SparseCore 0:
  37.2 40.8 reduce-scatter.4
  748.9 28.7 reduce-scatter.6
  1172.6 31.0 reduce-scatter.8
  1447.8 35.6 reduce-scatter.10
where the time goes:
time: 1500 us; the launch traced here: 1490 us
  blocking collectives  1270 us (85%)
  local copies, waits for them, and re-layouts  86.5 us (6%)
  between operations  36.6 us (2%)
  waiting for transfers between devices  34.1 us (2%)
  starting transfers between devices  26.5 us (2%)
  matrix products  26.5 us (2%)
  other arithmetic  16.8 us (1%)
    psum x4, blocking collectives, to_owners(): summed = lax.psum(partial_value, 'hours')  515 us
    unnamed x3, blocking collectives  390 us
    psum x3, blocking collectives, body(): dual_sum = lax.psum(dual_sq, ('hours', 'region'))  283 us
    all_gather x4, blocking collectives, body(): lax.all_gather(prices, 'region', axis=1, tiled=True)  77.2 us
    gather x3, local copies, waits for them, and re-layouts, body(): cap_dense = capacity_all[inverse].reshape(tech_count, node_count)  35.3 us
    gather x3, local copies, waits for them, and re-layouts, body(): jnp.sum(availability * cap_duals, axis=0).reshape(-1)[owner_cols]  35.3 us
    reduce_scatter x4, waiting for transfers between devices, body(): lax.psum_scatter(per_dest, 'region', scatter_dimension=1, tiled=True)  34 us
  transfers between devices with their start and end apart: 10, of which 1 were waited for; matrix products, arithmetic and copies ran while one was open for 7% of the time, Pallas kernels for 0%

commit v1 on v0

v1 whole, which is shorter than its diff:
```python
import functools

import jax
import jax.numpy as jnp
from jax import lax
from jax.experimental import pallas as pl
from jax.experimental.pallas import tpu as pltpu
from jax.sharding import PartitionSpec as P

ITERS = 4
PHASES = ITERS - 1
EPSILON = 1e-06
LANES = 128
WIDTH = 32
PARTS = 3
F32 = jnp.float32
BF16 = jnp.bfloat16
MESH = pl.DeviceIdType.MESH


def split(value, parts=PARTS):
    pieces = []
    for part in range(parts):
        piece = value.astype(BF16)
        pieces.append(piece)
        if part + 1 < parts:
            value = value - piece.astype(F32)
    return jnp.concatenate(pieces, axis=0)


def joined(value, parts=PARTS):
    rows = value.shape[0] // parts
    total = value[(parts - 1) * rows :]
    for part in range(parts - 2, -1, -1):
        total = total + value[part * rows : (part + 1) * rows]
    return total


def times(value, matrix):
    product = jnp.dot(split(value), matrix, preferred_element_type=F32)
    return joined(product)


def times_transposed(value, matrix):
    product = lax.dot_general(
        split(value), matrix, (((1,), (1,)), ((), ())), preferred_element_type=F32
    )
    return joined(product)


def fold(value):
    rows, cols = value.shape
    total = value[:, :LANES]
    for tile in range(1, cols // LANES):
        total = total + value[:, tile * LANES : (tile + 1) * LANES]
    if rows > 8:
        total = jnp.sum(total.reshape(rows // 8, 8, LANES), axis=0)
    return jnp.sum(total, axis=0, keepdims=True)


def wait_for(ref, sem):
    pltpu.make_async_copy(ref, ref, sem).wait()


def kernel(
    groups,
    avail,
    demand,
    gen,
    cost,
    owner,
    line_ends,
    line_limit,
    cross_ends,
    cross_limit,
    counts,
    store_node,
    energy,
    power,
    price_start,
    disp,
    cap_out,
    prices,
    charge,
    capd,
    inner,
    discharge,
    sdual,
    cross,
    bal,
    wide,
    local,
    ends_row,
    bound_row,
    msg,
    far,
    info_out,
    info_in,
    start_a,
    start_b,
    col_a,
    col_b,
    sq_a,
    sq_b,
    sq_c,
    halo_out,
    halo_in,
    pad_row,
    msg_send,
    msg_recv,
    info_send,
    info_recv,
    start_send,
    start_recv,
    col_send,
    col_recv,
    sq_send,
    sq_recv,
    halo_send,
    halo_recv,
):
    size_a, size_b, size_r = groups
    hours = size_a * size_b
    rows, tech, nodes = avail.shape
    half = rows // 2
    h = lax.axis_index("hours")
    r = lax.axis_index("region")
    in_a = lax.rem(h, size_a)
    in_b = lax.div(h, size_a)

    def device(hour, region):
        return {"hours": hour, "region": region}

    peers_a = [
        device(in_b * size_a + lax.rem(in_a + j, size_a), r) for j in range(1, size_a)
    ]
    peers_b = [
        device(lax.rem(in_b + j, size_b) * size_a + in_a, r) for j in range(1, size_b)
    ]
    peers_r = [device(h, lax.rem(r + j, size_r)) for j in range(1, size_r)]
    following = device(lax.rem(h + 1, hours), r)
    preceding = device(lax.rem(h + hours - 1, hours), r)

    barrier = pltpu.get_barrier_semaphore()
    everyone = peers_a + peers_b + peers_r + [following, preceding]
    for peer in everyone:
        pl.semaphore_signal(barrier, inc=1, device_id=peer, device_id_type=MESH)
    pl.semaphore_wait(barrier, len(everyone))

    def spread(slots, own, peers, send_sem, recv_sem):
        for peer in peers:
            pltpu.make_async_remote_copy(
                src_ref=slots.at[own],
                dst_ref=slots.at[own],
                send_sem=send_sem,
                recv_sem=recv_sem,
                device_id=peer,
                device_id_type=MESH,
            ).start()

    def collect(slots, peers, sem):
        wait_for(slots.at[pl.ds(0, len(peers))], sem)

    def total(slots):
        value = slots[0]
        for slot in range(1, slots.shape[0]):
            value = value + slots[slot]
        return value

    lane = lax.broadcasted_iota(jnp.int32, (1, LANES), 1)
    leaves = lax.rem(lane, 2 * WIDTH) < WIDTH

    for dest in range(size_r):
        tile = (dest * WIDTH) // LANES * LANES
        place = (dest * WIDTH) % LANES

        def placed(row, first):
            low = pltpu.roll(row, (first - place) % LANES, 1)
            high = pltpu.roll(row, (first + 2 * WIDTH - place) % LANES, 1)
            return jnp.where(lane < 2 * WIDTH, low, high)

        begins = cross_ends[0:1, tile : tile + LANES].astype(F32)
        finish = cross_ends[1:2, tile : tile + LANES].astype(F32)
        used = lax.rem(lane, WIDTH) < counts[0:1, dest : dest + 1]
        bound = jnp.where(used, cross_limit[0:1, tile : tile + LANES], 0.0)
        block = slice(dest * LANES, (dest + 1) * LANES)
        ends_row[:, block] = placed(begins, 0)
        bound_row[:, block] = placed(bound, 0)
        info_out[dest, 0:1] = placed(finish, WIDTH)
        info_out[dest, 1:2] = placed(bound, WIDTH)
    info_in[r] = jnp.zeros(info_in.shape[1:], F32)
    for j in range(1, size_r):
        dest = lax.rem(r + j, size_r)
        pltpu.make_async_remote_copy(
            src_ref=info_out.at[dest],
            dst_ref=info_in.at[r],
            send_sem=info_send,
            recv_sem=info_recv,
            device_id=device(h, dest),
            device_id_type=MESH,
        ).start()

    pad_row[...] = jnp.zeros((1, LANES), F32)
    owned = cost.shape[1]
    pad_row[:, 0:owned] = cost[...]
    per_tile = LANES // owned
    tile = pl.multiple_of(lax.div(h, per_tile) * LANES, LANES)
    cols = owner[0:1, pl.ds(tile, LANES)]
    where_in = lax.rem(h, per_tile)
    mine = cols
    for place in range(1, per_tile):
        moved = pltpu.roll(cols, (LANES - place * owned) % LANES, 1)
        mine = jnp.where(where_in == place, moved, mine)
    mine = jnp.where(lane < owned, mine, -1)
    col_tech = jnp.where(mine < 0, -1, lax.shift_right_arithmetic(mine, 7))
    col_node = jnp.where(mine < 0, -1, lax.rem(mine, nodes))
    node_iota = lax.broadcasted_iota(jnp.int32, (nodes, LANES), 0)
    tech_iota = lax.broadcasted_iota(jnp.int32, (tech, LANES), 0)
    col_hot = jnp.where(col_node == node_iota, 1.0, 0.0).astype(BF16)
    tech_hot = jnp.where(col_tech == tech_iota, 1.0, 0.0)
    start_a[in_a, tech:] = times_transposed(tech_hot * pad_row[...], col_hot)

    def add_hours(i, value):
        part = avail[pl.ds(i * 8, 8)]
        return value + jnp.sum(part, axis=0)

    start_a[in_a, :tech] = lax.fori_loop(
        0, rows // 8, add_hours, jnp.zeros((tech, nodes), F32)
    )
    spread(start_a, in_a, peers_a, start_send.at[0], start_recv.at[0])

    lines = line_limit.shape[1]
    units = energy.shape[1]
    line_iota = lax.broadcasted_iota(jnp.int32, (nodes, lines), 0)
    local[:, :lines] = (
        jnp.where(line_ends[1:2] == line_iota, 1.0, 0.0)
        - jnp.where(line_ends[0:1] == line_iota, 1.0, 0.0)
    ).astype(BF16)
    local[:, lines:] = jnp.where(store_node[...] == line_iota, 1.0, 0.0).astype(BF16)
    disp[...] = jnp.zeros(disp.shape, F32)
    capd[...] = jnp.zeros(capd.shape, F32)
    inner[...] = jnp.zeros(inner.shape, F32)
    discharge[...] = jnp.zeros(discharge.shape, F32)
    charge[...] = jnp.zeros(charge.shape, F32)
    sdual[...] = jnp.zeros(sdual.shape, F32)
    cross[...] = jnp.zeros(cross.shape, F32)
    prices[...] = price_start[...]

    collect(info_in, peers_r, info_recv)
    for dest in range(size_r):
        block = slice(dest * LANES, (dest + 1) * LANES)
        node_row = jnp.where(leaves, ends_row[:, block], info_in[dest, 0:1]).astype(jnp.int32)
        bound_row[:, block] = jnp.where(leaves, bound_row[:, block], info_in[dest, 1:2])
        hot = jnp.where(
            node_row == node_iota, jnp.where(leaves, -1.0, 1.0), 0.0
        )
        wide[:nodes, block] = jnp.where(lane < 2 * WIDTH, hot, 0.0).astype(BF16)
        wide[nodes:, block] = jnp.where(lane < 2 * WIDTH, 0.0, hot).astype(BF16)

    def send_duals(phase, values):
        packed = jnp.concatenate([values[:half], values[half:]], axis=1)
        near = times(packed, wide[...])
        for dest in range(size_r):
            msg[phase, dest] = near[:, dest * LANES : (dest + 1) * LANES]
        far[phase, r] = jnp.zeros((half, LANES), F32)
        for j in range(1, size_r):
            dest = lax.rem(r + j, size_r)
            pltpu.make_async_remote_copy(
                src_ref=msg.at[phase, dest],
                dst_ref=far.at[phase, r],
                send_sem=msg_send.at[phase],
                recv_sem=msg_recv.at[phase],
                device_id=device(h, dest),
                device_id_type=MESH,
            ).start()

    def slot_gaps(phase):
        collect(far.at[phase], peers_r, msg_recv.at[phase])
        gaps = []
        for dest in range(size_r):
            block = far[phase, dest]
            swapped = jnp.where(
                leaves, pltpu.roll(block, LANES - WIDTH, 1), pltpu.roll(block, WIDTH, 1)
            )
            gaps.append(swapped + msg[phase, dest])
        return jnp.concatenate(gaps, axis=1)

    send_duals(0, price_start[...])
    local_gaps = times(price_start[...], local[...])

    collect(start_a, peers_a, start_recv.at[0])
    start_b[in_b] = total(start_a)
    spread(start_b, in_b, peers_b, start_send.at[1], start_recv.at[1])
    gaps = slot_gaps(0)
    collect(start_b, peers_b, start_recv.at[1])
    both = total(start_b)
    col_weight, col_cost = both[:tech], both[tech:]

    capacity = jnp.zeros((tech, nodes), F32)
    pull = jnp.zeros((tech, nodes), F32)
    last_charge = jnp.zeros((1, units), F32)
    next_dual = jnp.zeros((1, units), F32)
    prev_dual = jnp.zeros((1, units), F32)
    weight = jnp.ones((1, 1), F32)
    unit_rows = lax.broadcasted_iota(jnp.int32, (rows, units), 0)

    for iteration in range(ITERS):
        final = iteration == ITERS - 1
        step = 0.5 / weight
        gap_line, gap_unit = local_gaps[:, :lines], local_gaps[:, lines:]
        bounds = bound_row[...]
        limit = line_limit[...]
        cross_old = cross[...]
        inner_old = inner[...]
        dis_old = discharge[...]
        charge_old = charge[...]
        sd_old = sdual[...]
        cross_new = jnp.clip(cross_old - step * gaps, -bounds, bounds)
        inner_new = jnp.clip(inner_old - step * gap_line, -limit, limit)
        dis_new = jnp.clip(dis_old - step * (gap_unit + sd_old), -power[...], power[...])
        sd_next = jnp.where(
            unit_rows == rows - 1, next_dual, pltpu.roll(sd_old, rows - 1, 0)
        )
        charge_new = jnp.clip(charge_old - step * (sd_old - sd_next), 0.0, energy[...])
        cross_gain = cross_new - cross_old
        inner_gain = inner_new - inner_old
        dis_gain = dis_new - dis_old
        dis_bar = dis_new + dis_gain
        charge[...] = charge_new
        net = times_transposed(cross_new + cross_gain, wide[...])
        flow = jnp.concatenate([inner_new + inner_gain, dis_bar], axis=1)
        bal[...] = (
            jnp.concatenate([net[:, :nodes], net[:, nodes:]], axis=0)
            + times_transposed(flow, local[...])
            - demand[...]
        )
        step_b = jnp.broadcast_to(step, (tech, nodes))
        gen_cost = gen[...]
        cap_new = jnp.maximum(capacity - (col_cost - pull) / (weight * col_weight), 0.0)
        cap_gain = cap_new - capacity
        capacity = cap_new

        if final:

            def last_hours(i, carry):
                here = pl.ds(i * 8, 8)
                old = disp[here]
                new = jnp.maximum(
                    old - step_b * (gen_cost + prices[here][:, None, :] + capd[here]), 0.0
                )
                bal[here] += jnp.sum(new + (new - old), axis=1)
                disp[here] = new
                return carry

            lax.fori_loop(0, rows // 8, last_hours, 0)
            prices[...] = prices[...] + weight / (tech + 8.0) * bal[...]
            break

        cap_bar = cap_new + cap_gain
        half_weight = jnp.broadcast_to(weight / 2.0, (tech, nodes))

        def some_hours(i, carry):
            pull_sum, primal, dual = carry
            here = pl.ds(i * 8, 8)
            share = avail[here]
            old = disp[here]
            dual_old = capd[here]
            new = jnp.maximum(
                old - step_b * (gen_cost + prices[here][:, None, :] + dual_old), 0.0
            )
            gain = new - old
            bar = new + gain
            bal[here] += jnp.sum(bar, axis=1)
            dual_new = jnp.maximum(dual_old + half_weight * (bar - share * cap_bar), 0.0)
            dual_gain = dual_new - dual_old
            disp[here] = new
            capd[here] = dual_new
            return (
                pull_sum + jnp.sum(share * dual_new, axis=0),
                primal + jnp.sum(gain * gain, axis=0),
                dual + jnp.sum(dual_gain * dual_gain, axis=0),
            )

        zero = jnp.zeros((tech, nodes), F32)
        pull_sum, primal, dual = lax.fori_loop(0, rows // 8, some_hours, (zero, zero, zero))

        cross[...] = cross_new
        inner[...] = inner_new
        discharge[...] = dis_new
        charge_gain = charge_new - charge_old
        charge_bar = charge_new + charge_gain
        last_new = jnp.clip(last_charge - step * (prev_dual - sd_old[0:1]), 0.0, energy[...])
        last_bar = last_new + (last_new - last_charge)
        last_charge = last_new
        before = jnp.where(unit_rows == 0, last_bar, pltpu.roll(charge_bar, 1, 0))
        sd_gain = weight / 3.0 * (charge_bar - before + dis_bar)
        sd_new = sd_old + sd_gain
        sdual[...] = sd_new
        price_old = prices[...]
        price_new = price_old + weight / (tech + 8.0) * bal[...]
        prices[...] = price_new
        price_gain = price_new - price_old

        leaving = jnp.where(leaves, 1.0, 0.0)
        cross_sq = fold(cross_gain * cross_gain) * leaving
        primal_row = (
            fold(primal)
            + fold(cap_gain * cap_gain) * (1.0 / hours)
            + fold(inner_gain * inner_gain)
            + cross_sq
            + fold(dis_gain * dis_gain)
            + fold(charge_gain * charge_gain)
        )
        sd_step = sd_new - sd_old
        dual_row = fold(dual) + fold(price_gain * price_gain) + fold(sd_step * sd_step)
        sq_a[iteration, in_b, 0:1] = primal_row
        sq_a[iteration, in_b, 1:2] = dual_row
        spread(
            sq_a.at[iteration], in_b, peers_b, sq_send.at[iteration, 0], sq_recv.at[iteration, 0]
        )
        col_a[iteration, in_a] = pull_sum
        spread(
            col_a.at[iteration],
            in_a,
            peers_a,
            col_send.at[iteration, 0],
            col_recv.at[iteration, 0],
        )
        halo_out[iteration, 0] = sd_new[0:1]
        halo_out[iteration, 1] = sd_new[rows - 1 : rows]
        for side, peer in ((0, preceding), (1, following)):
            pltpu.make_async_remote_copy(
                src_ref=halo_out.at[iteration, side],
                dst_ref=halo_in.at[iteration, side],
                send_sem=halo_send.at[iteration, side],
                recv_sem=halo_recv.at[iteration, side],
                device_id=peer,
                device_id_type=MESH,
            ).start()
        send_duals(iteration + 1, price_new)

        collect(sq_a.at[iteration], peers_b, sq_recv.at[iteration, 0])
        sq_b[iteration, in_a] = total(sq_a.at[iteration])
        spread(
            sq_b.at[iteration], in_a, peers_a, sq_send.at[iteration, 1], sq_recv.at[iteration, 1]
        )
        collect(col_a.at[iteration], peers_a, col_recv.at[iteration, 0])
        col_b[iteration, in_b] = total(col_a.at[iteration])
        spread(
            col_b.at[iteration],
            in_b,
            peers_b,
            col_send.at[iteration, 1],
            col_recv.at[iteration, 1],
        )
        local_gaps = times(price_new, local[...])
        collect(sq_b.at[iteration], peers_a, sq_recv.at[iteration, 1])
        sq_c[iteration, r] = total(sq_b.at[iteration])
        spread(
            sq_c.at[iteration], r, peers_r, sq_send.at[iteration, 2], sq_recv.at[iteration, 2]
        )
        collect(col_b.at[iteration], peers_b, col_recv.at[iteration, 1])
        pull = total(col_b.at[iteration])
        gaps = slot_gaps(iteration + 1)
        wait_for(halo_in.at[iteration, 0], halo_recv.at[iteration, 0])
        wait_for(halo_in.at[iteration, 1], halo_recv.at[iteration, 1])
        next_dual = halo_in[iteration, 0]
        prev_dual = halo_in[iteration, 1]
        collect(sq_c.at[iteration], peers_r, sq_recv.at[iteration, 2])
        sums = jnp.sum(total(sq_c.at[iteration]), axis=1, keepdims=True)
        ratio = (sums[1:2] + EPSILON) / (sums[0:1] + EPSILON)
        weight = jnp.sqrt(weight * jnp.sqrt(ratio))

    picked = times(capacity, col_hot) * tech_hot
    cap_out[...] = jnp.sum(picked, axis=0, keepdims=True)[:, :owned]

    collect(info_in, peers_r, info_send)
    collect(start_a, peers_a, start_send.at[0])
    collect(start_b, peers_b, start_send.at[1])
    for phase in range(ITERS):
        collect(far.at[phase], peers_r, msg_send.at[phase])
    for phase in range(PHASES):
        collect(sq_a.at[phase], peers_b, sq_send.at[phase, 0])
        collect(sq_b.at[phase], peers_a, sq_send.at[phase, 1])
        collect(sq_c.at[phase], peers_r, sq_send.at[phase, 2])
        collect(col_a.at[phase], peers_a, col_send.at[phase, 0])
        collect(col_b.at[phase], peers_b, col_send.at[phase, 1])
        for side in range(2):
            wait_for(halo_out.at[phase, side], halo_send.at[phase, side])


def body(
    availability,
    demand,
    gen_cost,
    cap_cost,
    owner_map,
    line_ends,
    line_limit,
    cross_ends,
    cross_limit,
    pair_counts,
    store_node,
    store_energy,
    store_power,
    price_start,
):
    rows, tech, nodes = availability.shape
    lines = line_limit.shape[0]
    units = store_node.shape[0]
    regions = lax.axis_size("region")
    hours = lax.axis_size("hours")
    size_a = 8 if hours % 64 == 0 else 2
    size_b = hours // size_a
    half = rows // 2
    slots = regions * LANES
    dma = pltpu.SemaphoreType.DMA
    scratch = [
        pltpu.VMEM((rows, tech, nodes), F32),
        pltpu.VMEM((rows, lines), F32),
        pltpu.VMEM((rows, units), F32),
        pltpu.VMEM((rows, units), F32),
        pltpu.VMEM((half, slots), F32),
        pltpu.VMEM((rows, nodes), F32),
        pltpu.VMEM((2 * nodes, slots), BF16),
        pltpu.VMEM((nodes, lines + units), BF16),
        pltpu.VMEM((1, slots), F32),
        pltpu.VMEM((1, slots), F32),
        pltpu.VMEM((ITERS, regions, half, LANES), F32),
        pltpu.VMEM((ITERS, regions, half, LANES), F32),
        pltpu.VMEM((regions, 2, LANES), F32),
        pltpu.VMEM((regions, 2, LANES), F32),
        pltpu.VMEM((size_a, 2 * tech, nodes), F32),
        pltpu.VMEM((size_b, 2 * tech, nodes), F32),
        pltpu.VMEM((PHASES, size_a, tech, nodes), F32),
        pltpu.VMEM((PHASES, size_b, tech, nodes), F32),
        pltpu.VMEM((PHASES, size_b, 2, LANES), F32),
        pltpu.VMEM((PHASES, size_a, 2, LANES), F32),
        pltpu.VMEM((PHASES, regions, 2, LANES), F32),
        pltpu.VMEM((PHASES, 2, 1, units), F32),
        pltpu.VMEM((PHASES, 2, 1, units), F32),
        pltpu.VMEM((1, LANES), F32),
        dma((ITERS,)),
        dma((ITERS,)),
        dma(()),
        dma(()),
        dma((2,)),
        dma((2,)),
        dma((PHASES, 2)),
        dma((PHASES, 2)),
        dma((PHASES, 3)),
        dma((PHASES, 3)),
        dma((PHASES, 2)),
        dma((PHASES, 2)),
    ]
    vmem = pl.BlockSpec(memory_space=pltpu.VMEM)
    outs = pl.pallas_call(
        functools.partial(kernel, (size_a, size_b, regions)),
        out_shape=(
            jax.ShapeDtypeStruct((rows, tech, nodes), F32),
            jax.ShapeDtypeStruct(cap_cost.shape, F32),
            jax.ShapeDtypeStruct((rows, nodes), F32),
            jax.ShapeDtypeStruct((rows, units), F32),
        ),
        in_specs=[vmem] * 14,
        out_specs=(vmem,) * 4,
        scratch_shapes=scratch,
        compiler_params=pltpu.CompilerParams(
            collective_id=0, has_side_effects=True, vmem_limit_bytes=40 * 1024 * 1024
        ),
    )(
        availability,
        demand,
        gen_cost,
        cap_cost,
        owner_map,
        line_ends,
        line_limit[None],
        cross_ends[:, 0],
        cross_limit,
        pair_counts,
        store_node[None],
        store_energy[None],
        store_power[None],
        price_start,
    )
    return outs


def solution(mesh):
    placed = (
        P("hours", None, "region"),
        P("hours", "region"),
        P(None, "region"),
        P("region", "hours"),
        P("region", None),
        P(None, "region"),
        P("region"),
        P(None, "region", None),
        P("region", None),
        P("region", None),
        P("region"),
        P("region"),
        P("region"),
        P("hours", "region"),
    )
    return jax.shard_map(
        body,
        mesh=mesh,
        in_specs=placed,
        out_specs=(
            P("hours", None, "region"),
            P("region", "hours"),
            P("hours", "region"),
            P("hours", "region"),
        ),
        check_vma=False,
    )
```

time: 1500 us -> 79 us (0.05)
  blocking collectives: 1270 us -> 0 us
  local copies, waits for them, and re-layouts: 86.5 us -> 9.84 us
  Pallas kernels: 0 us -> 68 us
  between operations: 36.6 us -> 0.7 us
  waiting for transfers between devices: 34.1 us -> 0 us
  matrix products: 26.5 us -> 0 us
  starting transfers between devices: 26.5 us -> 0 us
  other arithmetic: 16.8 us -> 0 us
    psum x7 -> x0, blocking collectives: 798 us -> none  [the longest x4 515 us: to_owners(): summed = lax.psum(partial_value, 'hours')]
    unnamed x3 -> x0, blocking collectives: 390 us -> none
    gather x7 -> x0, local copies, waits for them, and re-layouts: 82.4 us -> none  [the longest x3 35.3 us: body(): cap_dense = capacity_all[inverse].reshape(tech_count, node_count)]
    all_gather x4 -> x0, blocking collectives: 77.2 us -> none  [body(): lax.all_gather(prices, 'region', axis=1, tiled=True)]
    pallas_call x0 -> x1, Pallas kernels: none -> 68 us  [body(): pl.pallas_call(functools.partial(kernel, (size_a, size_b, regions)), out_...]
    reduce_scatter x4 -> x0, waiting for transfers between devices: 34 us -> none  [body(): lax.psum_scatter(per_dest, 'region', scatter_dimension=1, tiled=True)]
    dot_general x32 -> x0, matrix products: 26.5 us -> none  [the longest x4 5.11 us: body(): per_dest = jnp.dot(cross_bar, reach_map, precision=highest)]
    ppermute x6 -> x0, starting transfers between devices: 26.3 us -> none  [shifted(): return lax.ppermute(value, axis, pairs)]
  transfers between devices with their start and end apart: 10 -> 0, of which waited for: 1 -> 0; matrix products, arithmetic and copies ran while one was open for 7% -> 0% of each run, Pallas kernels for 0% -> 0%
where the time goes in v1:
time: 79 us; the launch traced here: 78.5 us
  Pallas kernels  68 us (86%)
  local copies, waits for them, and re-layouts  9.84 us (12%)
    pallas_call x1, Pallas kernels, body(): pl.pallas_call(functools.partial(kernel, (size_a, size_b, regions)), out_...  68 us
    unnamed x31, local copies, waits for them, and re-layouts  9.84 us

profile of v1, /device:TPU:1, one launch (start us, length us, event | category | flops | bytes accessed | tf_op | source)
XLA Modules:
  0.0 78.5 jit_solution(6305405754968301862)
XLA Ops:
  0.6 0.0 copy-start.3
  0.6 0.0 copy-start.5
  0.7 0.0 copy-start.7
  0.7 0.0 copy-start.8
  0.7 0.7 copy.20
  1.4 0.0 copy-start.6
  1.4 0.0 copy-done.3
  1.4 0.0 copy-done.5
  1.4 0.0 copy-done.7
  1.4 0.0 copy-done.8
  1.4 0.6 copy-done.6
  2.1 0.0 copy-start
  2.1 1.0 %copy-done = f32[64,16,128]{2,1,0:T(8,128)S(1)} copy-done((f32[64,16,128]{2,1,0:T(8,128)S(1)}, f32[64,16,128]{2,1,0:T(8,128)}, u32[]{:S(2)}) %copy-start) | copy-done | bytes 524312
  3.1 0.0 copy-start.1
  3.1 0.8 copy-done.1
  3.9 0.0 copy-start.2
  3.9 0.8 copy-done.2
  4.6 0.0 copy-start.4
  4.6 0.7 copy-done.4
  5.3 0.0 copy-start.9
  5.3 0.7 copy-done.9
  6.0 0.0 copy-start.10
  6.0 0.7 copy-done.10
  6.7 0.0 copy-start.11
  6.7 0.7 copy-done.11
  7.3 0.0 copy-start.12
  7.3 0.7 copy-done.12
  8.0 68.0 %shard_map.165 = (f32[64,16,128]{2,1,0:T(8,128)S(1)}, f32[1,32]{1,0:T(1,128)S(1)}, f32[64,128]{1,0:T(8,128)S(1)}, f32[64,256]{1,0:T(8,128)S(1)}) custom-call(f32[64,16,128]{2,1,0:T(8,128)S(1)} %copy-done, f32[64,128]{1,0:T(8,128)S(1)} %copy-done.1, f32[16,128]{1,0:T(8,128)S(1)} %copy-done.3, f32[1,32]{1,0:T(1,128)S(1)} %copy-done.11, ...), custom_call_target="tpu_custom_call" | custom-call | tf_op jit(solution)/shard_map/pallas_call | solution.py:557
  75.9 0.8 %copy.25 = f32[64,16,128]{2,1,0:T(8,128)} copy(f32[64,16,128]{2,1,0:T(8,128)S(1)} %get-tuple-element.8) | data formatting | bytes 1048576
  76.7 0.5 copy.26
  77.3 0.6 copy.27
  77.9 0.6 copy.28
Async XLA Ops:
  0.6 0.8 copy-start.3
  0.6 0.7 copy-start.5
  0.7 0.7 copy-start.7
  0.7 0.7 copy-start.8
  1.4 0.7 copy-start.6
  2.1 1.0 %copy-start = (f32[64,16,128]{2,1,0:T(8,128)S(1)}, f32[64,16,128]{2,1,0:T(8,128)}, u32[]{:S(2)}) copy-start(f32[64,16,128]{2,1,0:T(8,128)} %avail.1) | copy-start | bytes 1572868
  3.1 0.8 copy-start.1
  3.9 0.8 copy-start.2
  4.6 0.7 copy-start.4
  5.3 0.7 copy-start.9
  6.0 0.7 copy-start.10
  6.7 0.7 copy-start.11
  7.3 0.7 copy-start.12

commit v2 on v1

v2 whole, which is shorter than its diff:
```python
import functools

import jax
import jax.numpy as jnp
from jax import lax
from jax.experimental import pallas as pl
from jax.experimental.pallas import tpu as pltpu
from jax.sharding import PartitionSpec as P

ITERS = 4
PHASES = ITERS - 1
PIECES = 4
EPSILON = 1e-06
LANES = 128
WIDTH = 32
PARTS = 3
F32 = jnp.float32
BF16 = jnp.bfloat16
MESH = pl.DeviceIdType.MESH


def split(value, parts=PARTS):
    pieces = []
    for part in range(parts):
        piece = value.astype(BF16)
        pieces.append(piece)
        if part + 1 < parts:
            value = value - piece.astype(F32)
    return jnp.concatenate(pieces, axis=0)


def joined(value, parts=PARTS):
    rows = value.shape[0] // parts
    total = value[(parts - 1) * rows :]
    for part in range(parts - 2, -1, -1):
        total = total + value[part * rows : (part + 1) * rows]
    return total


def times(value, matrix):
    product = jnp.dot(split(value), matrix, preferred_element_type=F32)
    return joined(product)


def times_transposed(value, matrix):
    product = lax.dot_general(
        split(value), matrix, (((1,), (1,)), ((), ())), preferred_element_type=F32
    )
    return joined(product)


def fold(value):
    rows, cols = value.shape
    total = value[:, :LANES]
    for tile in range(1, cols // LANES):
        total = total + value[:, tile * LANES : (tile + 1) * LANES]
    if rows > 8:
        total = jnp.sum(total.reshape(rows // 8, 8, LANES), axis=0)
    return jnp.sum(total, axis=0, keepdims=True)


def wait_for(ref, sem):
    pltpu.make_async_copy(ref, ref, sem).wait()


def kernel(groups, *refs):
    sources, results, inputs = refs[:14], refs[14:18], refs[18:32]
    steps(groups, sources, results, inputs, *inputs, *refs[32:])


def steps(
    groups,
    sources,
    results,
    inputs,
    avail,
    demand,
    gen,
    cost,
    owner,
    line_ends,
    line_limit,
    cross_ends,
    cross_limit,
    counts,
    store_node,
    energy,
    power,
    price_start,
    in_sem,
    out_sem,
    disp,
    cap_row,
    prices,
    charge,
    capd,
    slope,
    inner,
    discharge,
    sdual,
    cross,
    bal,
    wide,
    wide_far,
    local,
    ends_row,
    far_row,
    bound_row,
    raw,
    msg,
    far,
    info_out,
    info_in,
    start_a,
    start_b,
    col_a,
    col_b,
    sq_a,
    sq_b,
    halo_out,
    halo_in,
    pad_row,
    raw_send,
    raw_recv,
    msg_send,
    msg_recv,
    info_send,
    info_recv,
    start_send,
    start_recv,
    col_send,
    col_recv,
    sq_send,
    sq_recv,
    halo_send,
    halo_recv,
):
    size_x, size_z, size_r = groups
    cores = 2
    size_a, size_b = size_x * cores, size_z
    hours = size_a * size_b
    rows, tech, nodes = avail.shape
    half = rows // 2
    h = lax.axis_index("hours")
    r = lax.axis_index("region")
    core = lax.rem(h, cores)
    in_a = lax.rem(h, size_a)
    in_x = lax.div(in_a, cores)
    in_b = lax.div(h, size_a)

    def device(hour, region):
        return {"hours": hour, "region": region}

    def others(first, second):
        def hops(step):
            return min(step[0], first - step[0]) + min(step[1], second - step[1])

        pairs = [(i, j) for i in range(first) for j in range(second) if i or j]
        return sorted(pairs, key=hops, reverse=True)

    peers_a = [
        device(in_b * size_a + lax.rem(in_a + j, size_a), r) for j in range(1, size_a)
    ]
    peers_b = [
        device(lax.rem(in_b + j, size_b) * size_a + in_a, r) for j in range(1, size_b)
    ]
    peers_r = [device(h, lax.rem(r + j, size_r)) for j in range(1, size_r)]
    peers_zx = [
        device(
            lax.rem(in_b + i, size_z) * size_a + lax.rem(in_x + j, size_x) * cores + core, r
        )
        for i, j in others(size_z, size_x)
    ]
    peers_rc = [
        device(h - core + lax.rem(core + j, cores), lax.rem(r + i, size_r))
        for i, j in others(size_r, cores)
    ]
    following = device(lax.rem(h + 1, hours), r)
    preceding = device(lax.rem(h + hours - 1, hours), r)

    barrier = pltpu.get_barrier_semaphore()
    everyone = peers_zx + peers_rc + peers_a + [following, preceding]
    for peer in everyone:
        pl.semaphore_signal(barrier, inc=1, device_id=peer, device_id_type=MESH)
    arriving = [
        pltpu.make_async_copy(source, target, in_sem.at[place])
        for place, (source, target) in enumerate(zip(sources, inputs))
    ]
    early = (0, 7, 8, 9, 3, 4)
    late = [place for place in range(len(inputs)) if place not in early]
    for place in (*early, *late):
        arriving[place].start()

    def spread(slots, own, peers, send_sem, recv_sem):
        for peer in peers:
            pltpu.make_async_remote_copy(
                src_ref=slots.at[own],
                dst_ref=slots.at[own],
                send_sem=send_sem,
                recv_sem=recv_sem,
                device_id=peer,
                device_id_type=MESH,
            ).start()

    def collect(slots, peers, sem):
        wait_for(slots.at[pl.ds(0, len(peers))], sem)

    def total(slots):
        values = [slots[slot] for slot in range(slots.shape[0])]
        while len(values) > 1:
            values = [
                sum(values[at + 1 : at + 2], values[at]) for at in range(0, len(values), 2)
            ]
        return values[0]

    lane = lax.broadcasted_iota(jnp.int32, (1, LANES), 1)
    leaves = lax.rem(lane, 2 * WIDTH) < WIDTH

    for place in early:
        arriving[place].wait()
    for dest in range(size_r):
        tile = (dest * WIDTH) // LANES * LANES
        place = (dest * WIDTH) % LANES

        def placed(row, first):
            low = pltpu.roll(row, (first - place) % LANES, 1)
            high = pltpu.roll(row, (first + 2 * WIDTH - place) % LANES, 1)
            return jnp.where(lane < 2 * WIDTH, low, high)

        begins = cross_ends[0, :, tile : tile + LANES].astype(F32)
        finish = cross_ends[1, :, tile : tile + LANES].astype(F32)
        used = lax.rem(lane, WIDTH) < counts[0:1, dest : dest + 1]
        bound = jnp.where(used, cross_limit[0:1, tile : tile + LANES], 0.0)
        block = slice(dest * LANES, (dest + 1) * LANES)
        ends_row[:, block] = placed(begins, 0)
        far_row[:, block] = placed(finish, 0)
        bound_row[:, block] = placed(bound, 0)
        info_out[dest, 0:1] = placed(finish, WIDTH)
        info_out[dest, 1:2] = placed(bound, WIDTH)
        info_out[dest, 2:3] = placed(begins, WIDTH)
        info_out[dest, 3:4] = jnp.zeros((1, LANES), F32)
    info_in[r] = jnp.zeros(info_in.shape[1:], F32)
    raw[r] = jnp.zeros(raw.shape[1:], F32)

    pad_row[...] = jnp.zeros((1, LANES), F32)
    owned = cost.shape[1]
    pad_row[:, 0:owned] = cost[...]
    per_tile = LANES // owned
    tile = pl.multiple_of(lax.div(h, per_tile) * LANES, LANES)
    cols = owner[0:1, pl.ds(tile, LANES)]
    where_in = lax.rem(h, per_tile)
    mine = cols
    for place in range(1, per_tile):
        moved = pltpu.roll(cols, (LANES - place * owned) % LANES, 1)
        mine = jnp.where(where_in == place, moved, mine)
    mine = jnp.where(lane < owned, mine, -1)
    col_tech = jnp.where(mine < 0, -1, lax.shift_right_arithmetic(mine, 7))
    col_node = jnp.where(mine < 0, -1, lax.rem(mine, nodes))
    node_iota = lax.broadcasted_iota(jnp.int32, (nodes, LANES), 0)
    tech_iota = lax.broadcasted_iota(jnp.int32, (tech, LANES), 0)
    col_hot = jnp.where(col_node == node_iota, 1.0, 0.0).astype(BF16)
    tech_hot = jnp.where(col_tech == tech_iota, 1.0, 0.0)
    start_a[in_a, tech:] = times_transposed(tech_hot * pad_row[...], col_hot)

    def add_hours(i, value):
        part = avail[pl.ds(i * 8, 8)]
        return value + jnp.sum(part, axis=0)

    start_a[in_a, :tech] = lax.fori_loop(
        0, rows // 8, add_hours, jnp.zeros((tech, nodes), F32)
    )

    pl.semaphore_wait(barrier, len(everyone))
    spread(start_a, in_a, peers_a, start_send.at[0], start_recv.at[0])
    for j in range(1, size_r):
        dest = lax.rem(r + j, size_r)
        pltpu.make_async_remote_copy(
            src_ref=info_out.at[dest],
            dst_ref=info_in.at[r],
            send_sem=info_send,
            recv_sem=info_recv,
            device_id=device(h, dest),
            device_id_type=MESH,
        ).start()
    for peer in peers_r:
        pltpu.make_async_remote_copy(
            src_ref=sources[13],
            dst_ref=raw.at[r],
            send_sem=raw_send,
            recv_sem=raw_recv,
            device_id=peer,
            device_id_type=MESH,
        ).start()
    for place in late:
        arriving[place].wait()

    lines = line_limit.shape[1]
    units = energy.shape[1]
    line_iota = lax.broadcasted_iota(jnp.int32, (nodes, lines), 0)
    local[:, :lines] = (
        jnp.where(line_ends[1:2] == line_iota, 1.0, 0.0)
        - jnp.where(line_ends[0:1] == line_iota, 1.0, 0.0)
    ).astype(BF16)
    local[:, lines:] = jnp.where(store_node[...] == line_iota, 1.0, 0.0).astype(BF16)
    local_gaps = times(price_start[...], local[...])

    def first_dispatch(i, primal):
        here = pl.ds(i * 8, 8)
        new = jnp.maximum(-0.5 * (gen[...] + price_start[here][:, None, :]), 0.0)
        disp[here] = new
        bal[here] = jnp.sum(new + new, axis=1) - demand[here]
        return primal + jnp.sum(new * new, axis=0)

    zero = jnp.zeros((tech, nodes), F32)
    primal = lax.fori_loop(0, rows // 8, first_dispatch, zero)

    collect(start_a, peers_a, start_recv.at[0])
    start_b[in_b] = total(start_a)
    spread(start_b, in_b, peers_b, start_send.at[1], start_recv.at[1])

    collect(info_in, peers_r, info_recv)
    for dest in range(size_r):
        block = slice(dest * LANES, (dest + 1) * LANES)
        near_at = jnp.where(leaves, ends_row[:, block], info_in[dest, 0:1]).astype(jnp.int32)
        far_at = jnp.where(leaves, far_row[:, block], info_in[dest, 2:3]).astype(jnp.int32)
        bound_row[:, block] = jnp.where(leaves, bound_row[:, block], info_in[dest, 1:2])
        sign = jnp.where(leaves, -1.0, 1.0)
        hot = jnp.where(near_at == node_iota, sign, 0.0)
        wide[:nodes, block] = jnp.where(lane < 2 * WIDTH, hot, 0.0).astype(BF16)
        wide[nodes:, block] = jnp.where(lane < 2 * WIDTH, 0.0, hot).astype(BF16)
        hot = jnp.where(far_at == node_iota, -sign, 0.0)
        wide_far[:nodes, block] = jnp.where(lane < 2 * WIDTH, hot, 0.0).astype(BF16)
        wide_far[nodes:, block] = jnp.where(lane < 2 * WIDTH, 0.0, hot).astype(BF16)

    def packed(values):
        return jnp.concatenate([values[:half], values[half:]], axis=1)

    near = times(packed(price_start[...]), wide[...])
    collect(raw, peers_r, raw_recv)
    gaps = near + jnp.concatenate(
        [
            times(packed(raw[dest]), wide_far[:, dest * LANES : (dest + 1) * LANES])
            for dest in range(size_r)
        ],
        axis=1,
    )

    def send_duals(phase, values):
        near = times(packed(values), wide[...])
        for dest in range(size_r):
            msg[phase, dest] = near[:, dest * LANES : (dest + 1) * LANES]
        far[phase, r] = jnp.zeros((half, LANES), F32)
        for j in range(1, size_r):
            dest = lax.rem(r + j, size_r)
            pltpu.make_async_remote_copy(
                src_ref=msg.at[phase, dest],
                dst_ref=far.at[phase, r],
                send_sem=msg_send.at[phase],
                recv_sem=msg_recv.at[phase],
                device_id=device(h, dest),
                device_id_type=MESH,
            ).start()

    def slot_gaps(phase):
        collect(far.at[phase], peers_r, msg_recv.at[phase])
        gaps = []
        for dest in range(size_r):
            block = far[phase, dest]
            swapped = jnp.where(
                leaves, pltpu.roll(block, LANES - WIDTH, 1), pltpu.roll(block, WIDTH, 1)
            )
            gaps.append(swapped + msg[phase, dest])
        return jnp.concatenate(gaps, axis=1)

    capacity = zero
    pull = zero
    last_charge = jnp.zeros((1, units), F32)
    next_dual = jnp.zeros((1, units), F32)
    prev_dual = jnp.zeros((1, units), F32)
    weight = jnp.ones((1, 1), F32)
    unit_rows = lax.broadcasted_iota(jnp.int32, (rows, units), 0)
    cross_old = jnp.zeros(cross.shape, F32)
    inner_old = jnp.zeros(inner.shape, F32)
    dis_old = jnp.zeros(discharge.shape, F32)
    charge_old = jnp.zeros(charge.shape, F32)
    sd_old = jnp.zeros(sdual.shape, F32)
    price_old = price_start[...]

    for iteration in range(ITERS):
        start = iteration == 0
        final = iteration == ITERS - 1
        step = 0.5 / weight
        gap_line, gap_unit = local_gaps[:, :lines], local_gaps[:, lines:]
        bounds = bound_row[...]
        limit = line_limit[...]
        if not start:
            cross_old = cross[...]
            inner_old = inner[...]
            dis_old = discharge[...]
            charge_old = charge[...]
            sd_old = sdual[...]
            price_old = prices[...]
        cross_new = jnp.clip(cross_old - step * gaps, -bounds, bounds)
        inner_new = jnp.clip(inner_old - step * gap_line, -limit, limit)
        dis_new = jnp.clip(dis_old - step * (gap_unit + sd_old), -power[...], power[...])
        sd_next = jnp.where(
            unit_rows == rows - 1, next_dual, pltpu.roll(sd_old, rows - 1, 0)
        )
        charge_new = jnp.clip(charge_old - step * (sd_old - sd_next), 0.0, energy[...])
        cross_gain = cross_new - cross_old
        inner_gain = inner_new - inner_old
        dis_gain = dis_new - dis_old
        dis_bar = dis_new + dis_gain
        charge[...] = charge_new
        net = times_transposed(cross_new + cross_gain, wide[...])
        flow = jnp.concatenate([inner_new + inner_gain, dis_bar], axis=1)
        moved = jnp.concatenate(
            [net[:, :nodes], net[:, nodes:]], axis=0
        ) + times_transposed(flow, local[...])
        step_b = jnp.broadcast_to(step, (tech, nodes))

        def new_capacity():
            return jnp.maximum(capacity - (col_cost - pull) / (weight * col_weight), 0.0)

        if final:
            pltpu.make_async_copy(charge, results[3], out_sem.at[3]).start()
            capacity = new_capacity()
            picked = times(capacity, col_hot) * tech_hot
            cap_row[...] = jnp.sum(picked, axis=0, keepdims=True)[:, :owned]
            pltpu.make_async_copy(cap_row, results[1], out_sem.at[1]).start()

            def last_hours(i, carry):
                here = pl.ds(i * 8, 8)
                old = disp[here]
                new = jnp.maximum(old - step_b * slope[here], 0.0)
                bal[here] = jnp.sum(new + (new - old), axis=1) - demand[here]
                disp[here] = new
                pltpu.make_async_copy(
                    disp.at[here], results[0].at[here], out_sem.at[0]
                ).start()
                return carry

            lax.fori_loop(0, rows // 8, last_hours, 0)
            prices[...] = price_old + weight / (tech + 8.0) * (bal[...] + moved)
            pltpu.make_async_copy(prices, results[2], out_sem.at[2]).start()
            break

        half_weight = jnp.broadcast_to(weight / 2.0, (tech, nodes))
        if start:
            price_new = price_old + weight / (tech + 8.0) * (bal[...] + moved)
            send_duals(1, price_new)
            collect(start_b, peers_b, start_recv.at[1])
            both = total(start_b)
            col_weight, col_cost = both[:tech], both[tech:]
            cap_new = new_capacity()
            cap_gain = cap_new - capacity
            cap_bar = cap_new + cap_gain

            def first_duals(i, dual):
                here = pl.ds(i * 8, 8)
                new = disp[here]
                dual_new = jnp.maximum(
                    half_weight * (new + new - avail[here] * cap_bar), 0.0
                )
                capd[here] = dual_new
                return dual + jnp.sum(dual_new * dual_new, axis=0)

            dual = lax.fori_loop(0, rows // 8, first_duals, zero)
        else:
            cap_new = new_capacity()
            cap_gain = cap_new - capacity
            cap_bar = cap_new + cap_gain

            def some_hours(i, carry):
                primal, dual = carry
                here = pl.ds(i * 8, 8)
                old = disp[here]
                dual_old = capd[here]
                new = jnp.maximum(old - step_b * slope[here], 0.0)
                gain = new - old
                bar = new + gain
                bal[here] = jnp.sum(bar, axis=1) - demand[here]
                dual_new = jnp.maximum(
                    dual_old + half_weight * (bar - avail[here] * cap_bar), 0.0
                )
                dual_gain = dual_new - dual_old
                disp[here] = new
                capd[here] = dual_new
                return (
                    primal + jnp.sum(gain * gain, axis=0),
                    dual + jnp.sum(dual_gain * dual_gain, axis=0),
                )

            primal, dual = lax.fori_loop(0, rows // 8, some_hours, (zero, zero))
            price_new = price_old + weight / (tech + 8.0) * (bal[...] + moved)

        capacity = cap_new
        charge_gain = charge_new - charge_old
        charge_bar = charge_new + charge_gain
        last_new = jnp.clip(last_charge - step * (prev_dual - sd_old[0:1]), 0.0, energy[...])
        last_bar = last_new + (last_new - last_charge)
        last_charge = last_new
        before = jnp.where(unit_rows == 0, last_bar, pltpu.roll(charge_bar, 1, 0))
        sd_gain = weight / 3.0 * (charge_bar - before + dis_bar)
        sd_new = sd_old + sd_gain
        price_gain = price_new - price_old

        leaving = jnp.where(leaves, 1.0, 0.0)
        cross_sq = fold(cross_gain * cross_gain) * leaving
        primal_row = (
            fold(primal)
            + fold(cap_gain * cap_gain) * (1.0 / hours)
            + fold(inner_gain * inner_gain)
            + cross_sq
            + fold(dis_gain * dis_gain)
            + fold(charge_gain * charge_gain)
        )
        sd_step = sd_new - sd_old
        dual_row = fold(dual) + fold(price_gain * price_gain) + fold(sd_step * sd_step)
        in_zx = in_b * size_x + in_x
        sq_a[iteration, in_zx, 0:1] = primal_row
        sq_a[iteration, in_zx, 1:2] = dual_row
        spread(
            sq_a.at[iteration],
            in_zx,
            peers_zx,
            sq_send.at[iteration, 0],
            sq_recv.at[iteration, 0],
        )

        cross[...] = cross_new
        inner[...] = inner_new
        discharge[...] = dis_new
        sdual[...] = sd_new
        prices[...] = price_new

        def prepare(i, pull_sum):
            here = pl.ds(i * 8, 8)
            dual_now = capd[here]
            slope[here] = gen[...] + prices[here][:, None, :] + dual_now
            return pull_sum + jnp.sum(avail[here] * dual_now, axis=0)

        col_a[iteration, in_a] = lax.fori_loop(0, rows // 8, prepare, zero)
        spread(
            col_a.at[iteration],
            in_a,
            peers_a,
            col_send.at[iteration, 0],
            col_recv.at[iteration, 0],
        )
        halo_out[iteration, 0] = sd_new[0:1]
        halo_out[iteration, 1] = sd_new[rows - 1 : rows]
        for side, peer in ((0, preceding), (1, following)):
            pltpu.make_async_remote_copy(
                src_ref=halo_out.at[iteration, side],
                dst_ref=halo_in.at[iteration, side],
                send_sem=halo_send.at[iteration, side],
                recv_sem=halo_recv.at[iteration, side],
                device_id=peer,
                device_id_type=MESH,
            ).start()
        if not start:
            send_duals(iteration + 1, price_new)
        local_gaps = times(price_new, local[...])

        collect(col_a.at[iteration], peers_a, col_recv.at[iteration, 0])
        col_b[iteration, in_b] = total(col_a.at[iteration])
        spread(
            col_b.at[iteration],
            in_b,
            peers_b,
            col_send.at[iteration, 1],
            col_recv.at[iteration, 1],
        )
        collect(sq_a.at[iteration], peers_zx, sq_recv.at[iteration, 0])
        in_rc = r * cores + core
        sq_b[iteration, in_rc] = total(sq_a.at[iteration])
        spread(
            sq_b.at[iteration],
            in_rc,
            peers_rc,
            sq_send.at[iteration, 1],
            sq_recv.at[iteration, 1],
        )
        gaps = slot_gaps(iteration + 1)
        wait_for(halo_in.at[iteration, 0], halo_recv.at[iteration, 0])
        wait_for(halo_in.at[iteration, 1], halo_recv.at[iteration, 1])
        next_dual = halo_in[iteration, 0]
        prev_dual = halo_in[iteration, 1]
        collect(col_b.at[iteration], peers_b, col_recv.at[iteration, 1])
        pull = total(col_b.at[iteration])
        collect(sq_b.at[iteration], peers_rc, sq_recv.at[iteration, 1])
        sums = jnp.sum(total(sq_b.at[iteration]), axis=1, keepdims=True)
        ratio = (sums[1:2] + EPSILON) / (sums[0:1] + EPSILON)
        weight = jnp.sqrt(weight * jnp.sqrt(ratio))

    collect(info_in, peers_r, info_send)
    collect(raw, peers_r, raw_send)
    collect(start_a, peers_a, start_send.at[0])
    collect(start_b, peers_b, start_send.at[1])
    for phase in range(1, ITERS):
        collect(far.at[phase], peers_r, msg_send.at[phase])
    for phase in range(PHASES):
        collect(sq_a.at[phase], peers_zx, sq_send.at[phase, 0])
        collect(sq_b.at[phase], peers_rc, sq_send.at[phase, 1])
        collect(col_a.at[phase], peers_a, col_send.at[phase, 0])
        collect(col_b.at[phase], peers_b, col_send.at[phase, 1])
        for side in range(2):
            wait_for(halo_out.at[phase, side], halo_send.at[phase, side])
    for place, value in enumerate((disp, cap_row, prices, charge)):
        pltpu.make_async_copy(value, results[place], out_sem.at[place]).wait()


def store_outputs(*refs):
    sources, targets, held = refs[:4], refs[4:8], refs[8:12]
    in_sem, out_sem = refs[12:]
    rows = sources[0].shape[0]
    piece = rows // PIECES
    parts = [(0, pl.ds(at * piece, piece)) for at in range(PIECES)]
    parts += [(place, slice(None)) for place in (3, 2, 1)]
    loads, stores = [], []
    for at, (place, here) in enumerate(parts):
        source, target, stage = (
            ref if place else ref.at[here]
            for ref in (sources[place], targets[place], held[place])
        )
        loads.append(pltpu.make_async_copy(source, stage, in_sem.at[at]))
        stores.append(pltpu.make_async_copy(stage, target, out_sem.at[at]))
    for load in loads:
        load.start()
    for load, store in zip(loads, stores):
        load.wait()
        store.start()
    for store in stores:
        store.wait()


def body(
    availability,
    demand,
    gen_cost,
    cap_cost,
    owner_map,
    line_ends,
    line_limit,
    cross_ends,
    cross_limit,
    pair_counts,
    store_node,
    store_energy,
    store_power,
    price_start,
):
    rows, tech, nodes = availability.shape
    lines = line_limit.shape[0]
    units = store_node.shape[0]
    regions = lax.axis_size("region")
    hours = lax.axis_size("hours")
    size_a = 8 if hours % 64 == 0 else 2
    size_b = hours // size_a
    half = rows // 2
    slots = regions * LANES
    dma = pltpu.SemaphoreType.DMA
    arrays = (
        availability,
        demand,
        gen_cost,
        cap_cost,
        owner_map,
        line_ends,
        line_limit[None],
        cross_ends,
        cross_limit,
        pair_counts,
        store_node[None],
        store_energy[None],
        store_power[None],
        price_start,
    )
    scratch = [pltpu.VMEM(array.shape, array.dtype) for array in arrays] + [
        dma((len(arrays),)),
        dma((4,)),
        pltpu.VMEM((rows, tech, nodes), F32),
        pltpu.VMEM(cap_cost.shape, F32),
        pltpu.VMEM((rows, nodes), F32),
        pltpu.VMEM((rows, units), F32),
        pltpu.VMEM((rows, tech, nodes), F32),
        pltpu.VMEM((rows, tech, nodes), F32),
        pltpu.VMEM((rows, lines), F32),
        pltpu.VMEM((rows, units), F32),
        pltpu.VMEM((rows, units), F32),
        pltpu.VMEM((half, slots), F32),
        pltpu.VMEM((rows, nodes), F32),
        pltpu.VMEM((2 * nodes, slots), BF16),
        pltpu.VMEM((2 * nodes, slots), BF16),
        pltpu.VMEM((nodes, lines + units), BF16),
        pltpu.VMEM((1, slots), F32),
        pltpu.VMEM((1, slots), F32),
        pltpu.VMEM((1, slots), F32),
        pltpu.VMEM((regions, rows, nodes), F32),
        pltpu.VMEM((ITERS, regions, half, LANES), F32),
        pltpu.VMEM((ITERS, regions, half, LANES), F32),
        pltpu.VMEM((regions, 4, LANES), F32),
        pltpu.VMEM((regions, 4, LANES), F32),
        pltpu.VMEM((size_a, 2 * tech, nodes), F32),
        pltpu.VMEM((size_b, 2 * tech, nodes), F32),
        pltpu.VMEM((PHASES, size_a, tech, nodes), F32),
        pltpu.VMEM((PHASES, size_b, tech, nodes), F32),
        pltpu.VMEM((PHASES, hours // 2, 2, LANES), F32),
        pltpu.VMEM((PHASES, 2 * regions, 2, LANES), F32),
        pltpu.VMEM((PHASES, 2, 1, units), F32),
        pltpu.VMEM((PHASES, 2, 1, units), F32),
        pltpu.VMEM((1, LANES), F32),
        dma(()),
        dma(()),
        dma((ITERS,)),
        dma((ITERS,)),
        dma(()),
        dma(()),
        dma((2,)),
        dma((2,)),
        dma((PHASES, 2)),
        dma((PHASES, 2)),
        dma((PHASES, 2)),
        dma((PHASES, 2)),
        dma((PHASES, 2)),
        dma((PHASES, 2)),
    ]
    hbm = pl.BlockSpec(memory_space=pltpu.HBM)
    outs = pl.pallas_call(
        functools.partial(kernel, (size_a // 2, size_b, regions)),
        out_shape=(
            jax.ShapeDtypeStruct((rows, tech, nodes), F32),
            jax.ShapeDtypeStruct(cap_cost.shape, F32),
            jax.ShapeDtypeStruct((rows, nodes), F32),
            jax.ShapeDtypeStruct((rows, units), F32),
        ),
        in_specs=[hbm] * len(arrays),
        out_specs=(hbm,) * 4,
        scratch_shapes=scratch,
        compiler_params=pltpu.CompilerParams(
            collective_id=0, has_side_effects=True, vmem_limit_bytes=60 * 1024 * 1024
        ),
    )(*arrays)
    return pl.pallas_call(
        store_outputs,
        out_shape=tuple(jax.ShapeDtypeStruct(out.shape, F32) for out in outs),
        in_specs=[hbm] * 4,
        out_specs=(hbm,) * 4,
        scratch_shapes=[pltpu.VMEM(out.shape, F32) for out in outs]
        + [dma((PIECES + 3,)), dma((PIECES + 3,))],
    )(*outs)


def solution(mesh):
    placed = (
        P("hours", None, "region"),
        P("hours", "region"),
        P(None, "region"),
        P("region", "hours"),
        P("region", None),
        P(None, "region"),
        P("region"),
        P(None, "region", None),
        P("region", None),
        P("region", None),
        P("region"),
        P("region"),
        P("region"),
        P("hours", "region"),
    )
    return jax.shard_map(
        body,
        mesh=mesh,
        in_specs=placed,
        out_specs=(
            P("hours", None, "region"),
            P("region", "hours"),
            P("hours", "region"),
            P("hours", "region"),
        ),
        check_vma=False,
    )
```

time: 79 us -> 64.8 us (0.82)
  local copies, waits for them, and re-layouts: 9.84 us -> 0 us
  Pallas kernels: 68 us -> 64 us
    unnamed x31 -> x0, local copies, waits for them, and re-layouts: 9.84 us -> none
    pallas_call x1 -> x2, Pallas kernels: 68 us -> 64 us  [the longest x1 62.1 us: body(): pl.pallas_call(functools.partial(kernel, (size_a // 2, size_b, regions)),...]
where the time goes in v2:
time: 64.8 us; the launch traced here: 64.6 us
  Pallas kernels  64 us (99%)
    pallas_call x1, Pallas kernels, body(): pl.pallas_call(functools.partial(kernel, (size_a // 2, size_b, regions)),...  62.1 us
    pallas_call x1, Pallas kernels, body(): pl.pallas_call(store_outputs, out_shape=tuple((jax.ShapeDtypeStruct(out.s...  1.9 us

profile of v2, /device:TPU:1, one launch (start us, length us, event | category | flops | bytes accessed | tf_op | source)
XLA Modules:
  0.0 64.6 jit_solution(4238992335145242826)
XLA Ops:
  0.6 62.1 %shard_map.165 = (f32[64,16,128]{2,1,0:T(8,128)}, f32[1,32]{1,0:T(1,128)}, f32[64,128]{1,0:T(8,128)}, f32[64,256]{1,0:T(8,128)}) custom-call(f32[64,16,128]{2,1,0:T(8,128)} %refs_0_.1, f32[64,128]{1,0:T(8,128)} %refs_1_.1, f32[16,128]{1,0:T(8,128)} %refs_2_.1, f32[1,32]{1,0:T(1,128)} %refs_3_.1, s32[1,2048]{1,0:T(1,128)} %refs_4_.1, s32[2,256]{1,0:T(2,128)} %refs_5_.1, ...), custom_call_target="tpu_custom_call" | custom-call | tf_op jit(solution)/shard_map/pallas_call | solution.py:730
  62.8 1.9 %shard_map.166 = (f32[64,16,128]{2,1,0:T(8,128)}, f32[1,32]{1,0:T(1,128)}, f32[64,128]{1,0:T(8,128)}, f32[64,256]{1,0:T(8,128)}) custom-call(f32[64,16,128]{2,1,0:T(8,128)} %get-tuple-element.8.refs_0_, f32[1,32]{1,0:T(1,128)} %get-tuple-element.9.refs_1_, f32[64,128]{1,0:T(8,128)} %get-tuple-element.10.refs_2_, f32[64,256]{1,0:T(8,128)} %get-tuple-element.11.refs_3_), custom_call_target="tpu_custom_call" | custom-call | tf_op jit(solution)/shard_map/pallas_call | solution.py:745

commit v3 on v2

--- a/solution.py
+++ b/solution.py
@@ -9,7 +9,6 @@
 
 ITERS = 4
 PHASES = ITERS - 1
-PIECES = 4
 EPSILON = 1e-06
 LANES = 128
 WIDTH = 32
@@ -65,14 +64,14 @@
 
 def kernel(groups, *refs):
     sources, results, inputs = refs[:14], refs[14:18], refs[18:32]
-    steps(groups, sources, results, inputs, *inputs, *refs[32:])
+    steps(groups, sources, inputs, results, *inputs, *refs[32:])
 
 
 def steps(
     groups,
     sources,
+    inputs,
     results,
-    inputs,
     avail,
     demand,
     gen,
@@ -88,11 +87,6 @@
     power,
     price_start,
     in_sem,
-    out_sem,
-    disp,
-    cap_row,
-    prices,
-    charge,
     capd,
     slope,
     inner,
@@ -136,6 +130,7 @@
     halo_recv,
 ):
     size_x, size_z, size_r = groups
+    disp, cap_row, prices, charge = results
     cores = 2
     size_a, size_b = size_x * cores, size_z
     hours = size_a * size_b
@@ -179,16 +174,16 @@
     preceding = device(lax.rem(h + hours - 1, hours), r)
 
     barrier = pltpu.get_barrier_semaphore()
-    everyone = peers_zx + peers_rc + peers_a + [following, preceding]
+    everyone = peers_b + peers_rc + peers_a
     for peer in everyone:
         pl.semaphore_signal(barrier, inc=1, device_id=peer, device_id_type=MESH)
     arriving = [
         pltpu.make_async_copy(source, target, in_sem.at[place])
         for place, (source, target) in enumerate(zip(sources, inputs))
     ]
-    early = (0, 7, 8, 9, 3, 4)
-    late = [place for place in range(len(inputs)) if place not in early]
-    for place in (*early, *late):
+    early = (3, 4, 7, 8, 9)
+    late = [place for place in range(1, len(inputs)) if place not in early]
+    for place in (*early, 0, *late):
         arriving[place].start()
 
     def spread(slots, own, peers, send_sem, recv_sem):
@@ -262,13 +257,11 @@
     tech_hot = jnp.where(col_tech == tech_iota, 1.0, 0.0)
     start_a[in_a, tech:] = times_transposed(tech_hot * pad_row[...], col_hot)
 
-    def add_hours(i, value):
-        part = avail[pl.ds(i * 8, 8)]
-        return value + jnp.sum(part, axis=0)
-
-    start_a[in_a, :tech] = lax.fori_loop(
-        0, rows // 8, add_hours, jnp.zeros((tech, nodes), F32)
-    )
+    arriving[0].wait()
+    weights = zero = jnp.zeros((tech, nodes), F32)
+    for at in range(0, rows, 8):
+        weights = weights + jnp.sum(avail[at : at + 8], axis=0)
+    start_a[in_a, :tech] = weights
 
     pl.semaphore_wait(barrier, len(everyone))
     spread(start_a, in_a, peers_a, start_send.at[0], start_recv.at[0])
@@ -311,8 +304,7 @@
         bal[here] = jnp.sum(new + new, axis=1) - demand[here]
         return primal + jnp.sum(new * new, axis=0)
 
-    zero = jnp.zeros((tech, nodes), F32)
-    primal = lax.fori_loop(0, rows // 8, first_dispatch, zero)
+    primal = lax.fori_loop(0, rows // 8, first_dispatch, zero, unroll=True)
 
     collect(start_a, peers_a, start_recv.at[0])
     start_b[in_b] = total(start_a)
@@ -423,11 +415,9 @@
             return jnp.maximum(capacity - (col_cost - pull) / (weight * col_weight), 0.0)
 
         if final:
-            pltpu.make_async_copy(charge, results[3], out_sem.at[3]).start()
             capacity = new_capacity()
             picked = times(capacity, col_hot) * tech_hot
             cap_row[...] = jnp.sum(picked, axis=0, keepdims=True)[:, :owned]
-            pltpu.make_async_copy(cap_row, results[1], out_sem.at[1]).start()
 
             def last_hours(i, carry):
                 here = pl.ds(i * 8, 8)
@@ -435,20 +425,36 @@
                 new = jnp.maximum(old - step_b * slope[here], 0.0)
                 bal[here] = jnp.sum(new + (new - old), axis=1) - demand[here]
                 disp[here] = new
-                pltpu.make_async_copy(
-                    disp.at[here], results[0].at[here], out_sem.at[0]
-                ).start()
                 return carry
 
-            lax.fori_loop(0, rows // 8, last_hours, 0)
+            lax.fori_loop(0, rows // 8, last_hours, 0, unroll=True)
             prices[...] = price_old + weight / (tech + 8.0) * (bal[...] + moved)
-            pltpu.make_async_copy(prices, results[2], out_sem.at[2]).start()
             break
+
+        charge_gain = charge_new - charge_old
+        charge_bar = charge_new + charge_gain
+        last_new = jnp.clip(last_charge - step * (prev_dual - sd_old[0:1]), 0.0, energy[...])
+        last_bar = last_new + (last_new - last_charge)
+        last_charge = last_new
+        before = jnp.where(unit_rows == 0, last_bar, pltpu.roll(charge_bar, 1, 0))
+        sd_gain = weight / 3.0 * (charge_bar - before + dis_bar)
+        sd_new = sd_old + sd_gain
+        sd_step = sd_new - sd_old
+        primal_row = (
+            fold(inner_gain * inner_gain)
+            + fold(cross_gain * cross_gain) * jnp.where(leaves, 1.0, 0.0)
+            + fold(dis_gain * dis_gain)
+            + fold(charge_gain * charge_gain)
+        )
+        dual_row = fold(sd_step * sd_step)
 
         half_weight = jnp.broadcast_to(weight / 2.0, (tech, nodes))
         if start:
             price_new = price_old + weight / (tech + 8.0) * (bal[...] + moved)
             send_duals(1, price_new)
+            price_gain = price_new - price_old
+            primal_row += fold(primal)
+            dual_row += fold(price_gain * price_gain)
             collect(start_b, peers_b, start_recv.at[1])
             both = total(start_b)
             col_weight, col_cost = both[:tech], both[tech:]
@@ -465,7 +471,7 @@
                 capd[here] = dual_new
                 return dual + jnp.sum(dual_new * dual_new, axis=0)
 
-            dual = lax.fori_loop(0, rows // 8, first_duals, zero)
+            dual = lax.fori_loop(0, rows // 8, first_duals, zero, unroll=True)
         else:
             cap_new = new_capacity()
             cap_gain = cap_new - capacity
@@ -491,32 +497,15 @@
                     dual + jnp.sum(dual_gain * dual_gain, axis=0),
                 )
 
-            primal, dual = lax.fori_loop(0, rows // 8, some_hours, (zero, zero))
+            primal, dual = lax.fori_loop(0, rows // 8, some_hours, (zero, zero), unroll=True)
             price_new = price_old + weight / (tech + 8.0) * (bal[...] + moved)
+            price_gain = price_new - price_old
+            primal_row += fold(primal)
+            dual_row += fold(price_gain * price_gain)
 
         capacity = cap_new
-        charge_gain = charge_new - charge_old
-        charge_bar = charge_new + charge_gain
-        last_new = jnp.clip(last_charge - step * (prev_dual - sd_old[0:1]), 0.0, energy[...])
-        last_bar = last_new + (last_new - last_charge)
-        last_charge = last_new
-        before = jnp.where(unit_rows == 0, last_bar, pltpu.roll(charge_bar, 1, 0))
-        sd_gain = weight / 3.0 * (charge_bar - before + dis_bar)
-        sd_new = sd_old + sd_gain
-        price_gain = price_new - price_old
-
-        leaving = jnp.where(leaves, 1.0, 0.0)
-        cross_sq = fold(cross_gain * cross_gain) * leaving
-        primal_row = (
-            fold(primal)
-            + fold(cap_gain * cap_gain) * (1.0 / hours)
-            + fold(inner_gain * inner_gain)
-            + cross_sq
-            + fold(dis_gain * dis_gain)
-            + fold(charge_gain * charge_gain)
-        )
-        sd_step = sd_new - sd_old
-        dual_row = fold(dual) + fold(price_gain * price_gain) + fold(sd_step * sd_step)
+        primal_row += fold(cap_gain * cap_gain) * (1.0 / hours)
+        dual_row += fold(dual)
         in_zx = in_b * size_x + in_x
         sq_a[iteration, in_zx, 0:1] = primal_row
         sq_a[iteration, in_zx, 1:2] = dual_row
@@ -540,7 +529,7 @@
             slope[here] = gen[...] + prices[here][:, None, :] + dual_now
             return pull_sum + jnp.sum(avail[here] * dual_now, axis=0)
 
-        col_a[iteration, in_a] = lax.fori_loop(0, rows // 8, prepare, zero)
+        col_a[iteration, in_a] = lax.fori_loop(0, rows // 8, prepare, zero, unroll=True)
         spread(
             col_a.at[iteration],
             in_a,
@@ -607,32 +596,18 @@
         collect(col_b.at[phase], peers_b, col_send.at[phase, 1])
         for side in range(2):
             wait_for(halo_out.at[phase, side], halo_send.at[phase, side])
-    for place, value in enumerate((disp, cap_row, prices, charge)):
-        pltpu.make_async_copy(value, results[place], out_sem.at[place]).wait()
 
 
 def store_outputs(*refs):
-    sources, targets, held = refs[:4], refs[4:8], refs[8:12]
-    in_sem, out_sem = refs[12:]
-    rows = sources[0].shape[0]
-    piece = rows // PIECES
-    parts = [(0, pl.ds(at * piece, piece)) for at in range(PIECES)]
-    parts += [(place, slice(None)) for place in (3, 2, 1)]
-    loads, stores = [], []
-    for at, (place, here) in enumerate(parts):
-        source, target, stage = (
-            ref if place else ref.at[here]
-            for ref in (sources[place], targets[place], held[place])
-        )
-        loads.append(pltpu.make_async_copy(source, stage, in_sem.at[at]))
-        stores.append(pltpu.make_async_copy(stage, target, out_sem.at[at]))
-    for load in loads:
-        load.start()
-    for load, store in zip(loads, stores):
-        load.wait()
-        store.start()
-    for store in stores:
-        store.wait()
+    sources, targets, sem = refs[:4], refs[4:8], refs[8]
+    copies = [
+        pltpu.make_async_copy(source, target, sem.at[place])
+        for place, (source, target) in enumerate(zip(sources, targets))
+    ]
+    for copy in copies:
+        copy.start()
+    for copy in copies:
+        copy.wait()
 
 
 def body(
@@ -679,11 +654,6 @@
     )
     scratch = [pltpu.VMEM(array.shape, array.dtype) for array in arrays] + [
         dma((len(arrays),)),
-        dma((4,)),
-        pltpu.VMEM((rows, tech, nodes), F32),
-        pltpu.VMEM(cap_cost.shape, F32),
-        pltpu.VMEM((rows, nodes), F32),
-        pltpu.VMEM((rows, units), F32),
         pltpu.VMEM((rows, tech, nodes), F32),
         pltpu.VMEM((rows, tech, nodes), F32),
         pltpu.VMEM((rows, lines), F32),
@@ -727,16 +697,17 @@
         dma((PHASES, 2)),
     ]
     hbm = pl.BlockSpec(memory_space=pltpu.HBM)
+    vmem = pl.BlockSpec(memory_space=pltpu.VMEM)
     outs = pl.pallas_call(
         functools.partial(kernel, (size_a // 2, size_b, regions)),
         out_shape=(
-            jax.ShapeDtypeStruct((rows, tech, nodes), F32),
-            jax.ShapeDtypeStruct(cap_cost.shape, F32),
-            jax.ShapeDtypeStruct((rows, nodes), F32),
-            jax.ShapeDtypeStruct((rows, units), F32),
+            pltpu.VMEM((rows, tech, nodes), F32),
+            pltpu.VMEM(cap_cost.shape, F32),
+            pltpu.VMEM((rows, nodes), F32),
+            pltpu.VMEM((rows, units), F32),
         ),
         in_specs=[hbm] * len(arrays),
-        out_specs=(hbm,) * 4,
+        out_specs=(vmem,) * 4,
         scratch_shapes=scratch,
         compiler_params=pltpu.CompilerParams(
             collective_id=0, has_side_effects=True, vmem_limit_bytes=60 * 1024 * 1024
@@ -745,10 +716,10 @@
     return pl.pallas_call(
         store_outputs,
         out_shape=tuple(jax.ShapeDtypeStruct(out.shape, F32) for out in outs),
-        in_specs=[hbm] * 4,
+        in_specs=[vmem] * 4,
         out_specs=(hbm,) * 4,
-        scratch_shapes=[pltpu.VMEM(out.shape, F32) for out in outs]
-        + [dma((PIECES + 3,)), dma((PIECES + 3,))],
+        scratch_shapes=[dma((4,))],
+        compiler_params=pltpu.CompilerParams(vmem_limit_bytes=4 * 1024 * 1024),
     )(*outs)
 
 

time: 64.8 us -> 60.8 us (0.938)
  Pallas kernels: 64 us -> 60.1 us
    pallas_call x1, Pallas kernels: 62.1 us -> 59.2 us  [body(): pl.pallas_call(functools.partial(kernel, (size_a // 2, size_b, regions)),...]
    pallas_call x1, Pallas kernels: 1.9 us -> 0.85 us  [body(): pl.pallas_call(store_outputs, out_shape=tuple((jax.ShapeDtypeStruct(out.s...]
where the time goes in v3:
time: 60.8 us; the launch traced here: 60.7 us
  Pallas kernels  60.1 us (99%)
  between operations  0.64 us (1%)
    pallas_call x1, Pallas kernels, body(): pl.pallas_call(functools.partial(kernel, (size_a // 2, size_b, regions)),...  59.2 us

profile of v3, /device:TPU:1, one launch (start us, length us, event | category | flops | bytes accessed | tf_op | source)
XLA Modules:
  0.0 60.7 jit_solution(4450971294439014929)
XLA Ops:
  0.6 59.2 %shard_map.165 = (f32[64,16,128]{2,1,0:T(8,128)S(1)}, f32[1,32]{1,0:T(1,128)S(1)}, f32[64,128]{1,0:T(8,128)S(1)}, f32[64,256]{1,0:T(8,128)S(1)}) custom-call(f32[64,16,128]{2,1,0:T(8,128)} %refs_0_.1, f32[64,128]{1,0:T(8,128)} %refs_1_.1, f32[16,128]{1,0:T(8,128)} %refs_2_.1, f32[1,32]{1,0:T(1,128)} %refs_3_.1, s32[1,2048]{1,0:T(1,128)} %refs_4_.1, ...), custom_call_target="tpu_custom_call" | custom-call | tf_op jit(solution)/shard_map/pallas_call | solution.py:701
  59.8 0.9 %shard_map.166 = (f32[64,16,128]{2,1,0:T(8,128)}, f32[1,32]{1,0:T(1,128)}, f32[64,128]{1,0:T(8,128)}, f32[64,256]{1,0:T(8,128)}) custom-call(f32[64,16,128]{2,1,0:T(8,128)S(1)} %get-tuple-element.8.refs_0_, f32[1,32]{1,0:T(1,128)S(1)} %get-tuple-element.9.refs_1_, f32[64,128]{1,0:T(8,128)S(1)} %get-tuple-element.10.refs_2_, ...), custom_call_target="tpu_custom_call" | custom-call | tf_op jit(solution)/shard_map/pallas_call | solution.py:716

commit v4 on v3

--- a/solution.py
+++ b/solution.py
@@ -12,7 +12,7 @@
 EPSILON = 1e-06
 LANES = 128
 WIDTH = 32
-PARTS = 3
+PARTS = 2
 F32 = jnp.float32
 BF16 = jnp.bfloat16
 MESH = pl.DeviceIdType.MESH

time: 60.8 us -> 60.7 us (level)
  no operation moved by 1% of the time
where the time goes in v4:
time: 60.7 us; the launch traced here: 60.5 us
  Pallas kernels  59.9 us (99%)
  between operations  0.64 us (1%)
    pallas_call x1, Pallas kernels, body(): pl.pallas_call(functools.partial(kernel, (size_a // 2, size_b, regions)),...  59 us

profile of v4, /device:TPU:1, one launch (start us, length us, event | category | flops | bytes accessed | tf_op | source)
XLA Modules:
  0.0 60.5 jit_solution(4884328986360455820)
XLA Ops:
  0.6 59.0 %shard_map.165 = (f32[64,16,128]{2,1,0:T(8,128)S(1)}, f32[1,32]{1,0:T(1,128)S(1)}, f32[64,128]{1,0:T(8,128)S(1)}, f32[64,256]{1,0:T(8,128)S(1)}) custom-call(f32[64,16,128]{2,1,0:T(8,128)} %refs_0_.1, f32[64,128]{1,0:T(8,128)} %refs_1_.1, f32[16,128]{1,0:T(8,128)} %refs_2_.1, f32[1,32]{1,0:T(1,128)} %refs_3_.1, s32[1,2048]{1,0:T(1,128)} %refs_4_.1, ...), custom_call_target="tpu_custom_call" | custom-call | tf_op jit(solution)/shard_map/pallas_call | solution.py:701
  59.7 0.9 %shard_map.166 = (f32[64,16,128]{2,1,0:T(8,128)}, f32[1,32]{1,0:T(1,128)}, f32[64,128]{1,0:T(8,128)}, f32[64,256]{1,0:T(8,128)}) custom-call(f32[64,16,128]{2,1,0:T(8,128)S(1)} %get-tuple-element.8.refs_0_, f32[1,32]{1,0:T(1,128)S(1)} %get-tuple-element.9.refs_1_, f32[64,128]{1,0:T(8,128)S(1)} %get-tuple-element.10.refs_2_, ...), custom_call_target="tpu_custom_call" | custom-call | tf_op jit(solution)/shard_map/pallas_call | solution.py:716
